TPU v7x, 32 devices: a whole 2x2x4 slice. The times are simulated.
32 devices in a mesh: groups: 2 (over y), row: 4 (over z), col: 2 (over x), rep: 2 (over core).
Axes of the slice: x: 2, y: 2, z: 4, core: 2. Of those that a mesh axis runs over, the one named last changes fastest.
Arguments:
- density: float32 [256, 64, 64], P(('groups', 'row', 'col', 'rep')), parts along dimension 0, may hold values from -0.09 to 0.09
- left_index: int32 [2, 2, 256, 32], P(None, None, ('groups', 'row', 'col', 'rep')), parts along dimension 2, may hold values from 0 to 31
- right_index: int32 [2, 2, 256, 32], P(None, None, ('groups', 'row', 'col', 'rep')), parts along dimension 2, may hold values from 0 to 63
- pair_count: int32 [2, 2, 256], P(None, None, ('groups', 'row', 'col', 'rep')), parts along dimension 2, may hold values from 8 to 32, as said below
Outputs:
- purified: float32 [256, 64, 64], P(('groups', 'row', 'col', 'rep')), parts along dimension 0
There are 2 independent parts, one for each index of `groups`. A program takes and returns all parts, laid end to end along the dimension named above; each array names one. Nothing has to cross between parts.
Inputs may be any that keep to these rules, and one draw needn't show every extreme that they name: `pair_count`: each aligned group of 8 stored blocks has, for every step and product, one block with all 32 pairs live.
All inputs are finite; a program needn't handle non-finite values.
Results may differ from a plain program's by a relative error of at most 0.0003.
Values sent between devices are 32-bit elements; how exact they have to be, the bound alone decides.
No kernel may reach another device: no remote copies, remote signals or barrier semaphores. Data moves between devices by JAX's collectives and lax.ppermute only.
A program may use at most 128 MiB of HBM per device.

v0:
```python
import functools

import jax
import jax.numpy as jnp
from jax import lax
from jax.experimental import pallas as pl
from jax.experimental.pallas import tpu as pltpu
from jax.sharding import PartitionSpec as P

STEPS = 2
CODE = 256
CHUNK = 4
VMEM = pl.BlockSpec(memory_space=pltpu.VMEM)
ANY = pl.BlockSpec(memory_space=pl.ANY)
BF16 = jnp.bfloat16
F32 = jnp.float32


def middle_view(blocks):
    width = blocks.shape[1]
    padded = jnp.concatenate([blocks, jnp.zeros((1, width, width), blocks.dtype)], axis=0)
    return jnp.transpose(padded, (1, 0, 2))


def multiply(left_blocks, right_blocks, left_rows, right_rows, live_counts):
    slot_count, pair_width = left_rows.shape
    width = left_blocks.shape[1]
    left_view = middle_view(left_blocks)
    right_view = middle_view(right_blocks)
    positions = jnp.arange(pair_width, dtype=jnp.int32)
    live = positions[None, :] < live_counts[:, None]
    left_pick = jnp.where(live, left_rows, left_blocks.shape[0]).reshape(slot_count * pair_width)
    right_pick = jnp.where(live, right_rows, right_blocks.shape[0]).reshape(slot_count * pair_width)
    left_taken = jnp.take(left_view, left_pick, axis=1).reshape(
        width, slot_count, pair_width, width
    )
    right_taken = jnp.take(right_view, right_pick, axis=1).reshape(
        width, slot_count, pair_width, width
    )
    return jnp.einsum("iskj,jskl->sil", left_taken, right_taken, precision=lax.Precision.HIGHEST)


def panel_form(density, left_index, right_index, pair_count):
    current = density
    for step in range(STEPS):
        row_blocks = lax.all_gather(current, ("col", "rep"), axis=0, tiled=True)
        column_blocks = lax.all_gather(current, ("row", "rep"), axis=0, tiled=True)
        square = multiply(
            row_blocks,
            column_blocks,
            left_index[step, 0],
            right_index[step, 0],
            pair_count[step, 0],
        )
        square_rows = lax.all_gather(square, ("col", "rep"), axis=0, tiled=True)
        cube = multiply(
            square_rows,
            column_blocks,
            left_index[step, 1],
            right_index[step, 1],
            pair_count[step, 1],
        )
        current = 3.0 * square - 2.0 * cube
    return current


def left_lanes(rows):
    return lax.broadcasted_iota(jnp.int32, (rows, 128), 1) < 64


def spread(packed):
    turned = pltpu.roll(packed, 64, 1)
    left = left_lanes(32)
    return jnp.concatenate([jnp.where(left, packed, turned), jnp.where(left, turned, packed)], axis=0)


def pack(twice):
    return jnp.where(left_lanes(32), twice[:32], twice[32:])


def halves(twice):
    high = twice.astype(BF16)
    return high, twice - high.astype(F32)


def store_left(ref, at, twice):
    high, low = halves(twice)
    ref[at, 0:64] = high
    ref[at, 64:128] = low.astype(BF16)


def store_right(ref, at, twice):
    high, low = halves(twice)
    ref[at] = jnp.where(left_lanes(64), high.astype(F32), low).astype(BF16)


def prepare(source, first, count, base, left_ref, right_ref, unroll=8):
    def body(i, carry):
        twice = spread(source[first + i])
        if left_ref is not None:
            store_left(left_ref, base + i, twice)
        if right_ref is not None:
            store_right(right_ref, base + i, twice)
        return carry

    lax.fori_loop(0, count, body, 0, unroll=unroll)


def zero_block(left_ref, left_at, right_ref, right_at):
    if left_ref is not None:
        left_ref[left_at] = jnp.zeros((128, 128), BF16)
    if right_ref is not None:
        right_ref[right_at] = jnp.zeros((64, 128), BF16)


def filtered(codes, at, lane, pairs, left_ref, right_ref):
    mask = left_lanes(128)
    total = jnp.zeros((128, 128), F32)
    for start in range(0, pairs, CHUNK):
        lefts, rights = [], []
        for p in range(start, start + CHUNK):
            code = codes[at, lane + p]
            lefts.append(left_ref[(code >> 8) & (CODE - 1)])
            rights.append(right_ref[code & (CODE - 1)])
        left = jnp.concatenate(
            [jnp.where(mask, lefts[0], lefts[1]), jnp.where(mask, lefts[2], lefts[3])], axis=1
        )
        right = jnp.concatenate(rights, axis=0)
        total = total + jnp.dot(left, right, preferred_element_type=F32)
    both = total[:64] + total[64:]
    return both + pltpu.roll(both, 64, 1)


class Sizes:
    def __init__(self, mesh_shape, slots, pairs):
        self.rows, self.cols, self.reps = mesh_shape["row"], mesh_shape["col"], mesh_shape["rep"]
        self.slots, self.pairs = slots, pairs
        self.tile = self.reps * slots
        self.panel = self.cols * self.tile
        self.tiles = self.rows * self.cols
        self.blocks = self.tiles * self.tile
        self.half = self.tiles * slots


def pack_kernel(sizes, density, left_index, right_index, pair_count, out, blocks, lefts, rights, counts, sems):
    copies = [
        pltpu.make_async_copy(source, target, sems.at[i])
        for i, (source, target) in enumerate(
            ((density, blocks), (left_index, lefts), (right_index, rights), (pair_count, counts))
        )
    ]
    for copy in copies:
        copy.start()
    row, col = lax.axis_index("row"), lax.axis_index("col")
    for copy in copies[1:]:
        copy.wait()
    position = lax.broadcasted_iota(jnp.int32, (sizes.slots, sizes.pairs), 1)
    slot = lax.broadcasted_iota(jnp.int32, (sizes.slots, sizes.pairs), 0)
    codes = []
    for n in range(STEPS):
        for q in range(2):
            live = jnp.zeros((sizes.slots, sizes.pairs), jnp.int32)
            for s in range(sizes.slots):
                live = jnp.where(slot == s, counts[n, q, s], live)
            right = rights[n, q]
            inside = lax.rem(right, sizes.tile)
            left = lefts[n, q] + (row * sizes.panel if n == 0 else 0)
            right = (right - inside) * sizes.cols + col * sizes.tile + inside
            dead = position >= live
            left = jnp.where(dead, sizes.blocks if n == 0 else sizes.panel, left)
            right = jnp.where(dead, sizes.blocks, right)
            codes.append(((live * CODE + left) * CODE + right).astype(F32))
    out[sizes.slots * 32 : sizes.slots * 33] = jnp.concatenate(codes, axis=1)
    copies[0].wait()
    for s in range(sizes.slots):
        out[s * 32 : s * 32 + 32] = jnp.concatenate([blocks[s, :32], blocks[s, 32:]], axis=1)


def first_square_kernel(sizes, *refs):
    count = sizes.tiles * sizes.reps
    pieces, (out, right_ref, codes_out, left_ref, codes, sem) = refs[:count], refs[count:]
    row, col, rep = lax.axis_index("row"), lax.axis_index("col"), lax.axis_index("rep")
    places = []
    for e in range(sizes.reps):
        for m in range(sizes.rows):
            for n in range(sizes.cols):
                tile = (row ^ m) * sizes.cols + (col ^ n)
                places.append(pl.multiple_of(tile * sizes.tile + (rep ^ e) * sizes.slots, sizes.slots))
    for piece, base in zip(pieces, places):
        codes_out[pl.ds(base, sizes.slots)] = piece[sizes.slots * 32 : sizes.slots * 33].astype(jnp.int32)
    copy = pltpu.make_async_copy(codes_out, codes, sem)
    copy.start()
    zero_block(left_ref, sizes.blocks, right_ref, sizes.blocks)
    for piece, base in zip(pieces, places):
        for s in range(sizes.slots):
            twice = spread(piece[s * 32 : s * 32 + 32])
            store_left(left_ref, base + s, twice)
            store_right(right_ref, base + s, twice)
    copy.wait()

    def body(i, carry):
        base = (i * sizes.reps + rep) * sizes.slots
        for s in range(sizes.slots):
            out[i * sizes.slots + s] = pack(filtered(codes, base + s, 0, sizes.pairs, left_ref, right_ref))
        return carry

    lax.fori_loop(0, sizes.tiles, body, 0)


def first_cube_kernel(sizes, own, other, right_ref, codes_in, out, left_ref, codes, sem):
    copy = pltpu.make_async_copy(codes_in, codes, sem)
    copy.start()
    rep = lax.axis_index("rep")
    zero_block(left_ref, sizes.blocks, None, None)

    def prepare_tile(i, carry):
        for e, source in ((rep, own), (1 - rep, other)):
            for s in range(sizes.slots):
                store_left(
                    left_ref, (i * sizes.reps + e) * sizes.slots + s, spread(source[i * sizes.slots + s])
                )
        return carry

    lax.fori_loop(0, sizes.tiles, prepare_tile, 0)
    copy.wait()

    def body(i, carry):
        base = (i * sizes.reps + rep) * sizes.slots
        for s in range(sizes.slots):
            cube = pack(filtered(codes, base + s, sizes.pairs, sizes.pairs, left_ref, right_ref))
            out[i * sizes.slots + s] = 3.0 * own[i * sizes.slots + s] - 2.0 * cube
        return carry

    lax.fori_loop(0, sizes.tiles, body, 0)


def last_square_kernel(sizes, own, other, codes_in, out, right_ref, left_ref, codes, sem):
    copy = pltpu.make_async_copy(codes_in, codes, sem)
    copy.start()
    row, rep = lax.axis_index("row"), lax.axis_index("rep")
    zero_block(left_ref, sizes.panel, right_ref, sizes.blocks)

    def prepare_tile(i, carry):
        for e, source in ((rep, own), (1 - rep, other)):
            for s in range(sizes.slots):
                store_right(
                    right_ref, (i * sizes.reps + e) * sizes.slots + s, spread(source[i * sizes.slots + s])
                )
        return carry

    lax.fori_loop(0, sizes.tiles, prepare_tile, 0)
    for n in range(sizes.cols):
        for e, source in ((rep, own), (1 - rep, other)):
            for s in range(sizes.slots):
                twice = spread(source[(row * sizes.cols + n) * sizes.slots + s])
                store_left(left_ref, (n * sizes.reps + e) * sizes.slots + s, twice)
    copy.wait()

    def body(n, carry):
        base = row * sizes.panel + (n * sizes.reps + rep) * sizes.slots
        for s in range(sizes.slots):
            out[n * sizes.slots + s] = pack(
                filtered(codes, base + s, 2 * sizes.pairs, sizes.pairs, left_ref, right_ref)
            )
        return carry

    lax.fori_loop(0, sizes.cols, body, 0)


def last_cube_kernel(sizes, own, other, right_ref, codes_in, out, left_ref, codes, sem):
    copy = pltpu.make_async_copy(codes_in, codes, sem)
    copy.start()
    row, col, rep = lax.axis_index("row"), lax.axis_index("col"), lax.axis_index("rep")
    zero_block(left_ref, sizes.panel, None, None)
    for n in range(sizes.cols):
        for e, source in ((rep, own), (1 - rep, other)):
            for s in range(sizes.slots):
                twice = spread(source[n * sizes.slots + s])
                store_left(left_ref, (n * sizes.reps + e) * sizes.slots + s, twice)
    copy.wait()
    base = row * sizes.panel + (col * sizes.reps + rep) * sizes.slots
    for s in range(sizes.slots):
        cube = filtered(codes, base + s, 3 * sizes.pairs, sizes.pairs, left_ref, right_ref)
        square = spread(own[col * sizes.slots + s])
        out[s] = (3.0 * square - 2.0 * cube)[:, :64]


def call(kernel, sizes, outs, in_specs, out_specs, scratch, limit=40):
    return pl.pallas_call(
        functools.partial(kernel, sizes),
        out_shape=outs,
        in_specs=in_specs,
        out_specs=out_specs,
        scratch_shapes=scratch,
        compiler_params=pltpu.CompilerParams(vmem_limit_bytes=limit * 2**20),
    )


def whole_form(sizes, density, left_index, right_index, pair_count):
    width = density.shape[1]
    index_shape = (STEPS, 2, sizes.slots, sizes.pairs)
    code_shape = (sizes.blocks, STEPS * 2 * sizes.pairs)
    packed = lambda count: jax.ShapeDtypeStruct((count, 32, 128), F32)
    rights = jax.ShapeDtypeStruct((sizes.blocks + 1, 64, 128), BF16)
    code_scratch = [pltpu.SMEM(code_shape, jnp.int32), pltpu.SemaphoreType.DMA]

    payload = call(
        pack_kernel,
        sizes,
        jax.ShapeDtypeStruct((sizes.slots * 33, 128), F32),
        [ANY] * 4,
        VMEM,
        [
            pltpu.VMEM((sizes.slots, width, width), F32),
            pltpu.VMEM(index_shape, jnp.int32),
            pltpu.VMEM(index_shape, jnp.int32),
            pltpu.SMEM((STEPS, 2, sizes.slots), jnp.int32),
            pltpu.SemaphoreType.DMA((4,)),
        ],
    )(density, left_index, right_index, pair_count)

    def row_swap(value, m):
        return lax.ppermute(value, "row", [(i, i ^ m) for i in range(sizes.rows)])

    def both_swap(value, m):
        axes = ("row", "col")
        return lax.ppermute(value, axes, [(i, i ^ (2 * m + 1)) for i in range(2 * sizes.rows)])

    def col_swap(value):
        return lax.ppermute(value, "col", [(0, 1), (1, 0)])

    def rep_swap(value):
        return lax.ppermute(value, "rep", [(0, 1), (1, 0)])

    pieces = [payload, col_swap(payload)]
    for m in range(1, sizes.rows):
        arrived = row_swap(payload, m)
        pieces += [arrived, both_swap(payload, m) if m == 1 else col_swap(arrived)]
    pieces += [rep_swap(piece) for piece in pieces]

    square, right, codes = call(
        first_square_kernel,
        sizes,
        [packed(sizes.half), rights, jax.ShapeDtypeStruct(code_shape, jnp.int32)],
        [VMEM] * len(pieces),
        [VMEM] * 3,
        [pltpu.VMEM((sizes.blocks + 1, 128, 128), BF16)] + code_scratch,
    )(*pieces)
    current = call(
        first_cube_kernel,
        sizes,
        packed(sizes.half),
        [VMEM] * 3 + [ANY],
        VMEM,
        [pltpu.VMEM((sizes.blocks + 1, 128, 128), BF16)] + code_scratch,
    )(square, rep_swap(square), right, codes)
    square, right = call(
        last_square_kernel,
        sizes,
        [packed(sizes.cols * sizes.slots), rights],
        [VMEM] * 2 + [ANY],
        [VMEM] * 2,
        [pltpu.VMEM((sizes.panel + 1, 128, 128), BF16)] + code_scratch,
    )(current, rep_swap(current), codes)
    return call(
        last_cube_kernel,
        sizes,
        jax.ShapeDtypeStruct(density.shape, F32),
        [VMEM] * 3 + [ANY],
        VMEM,
        [pltpu.VMEM((sizes.panel + 1, 128, 128), BF16)] + code_scratch,
    )(square, rep_swap(square), right, codes)


def solution(mesh):
    def local(density, left_index, right_index, pair_count):
        sizes = Sizes(mesh.shape, density.shape[0], left_index.shape[3])
        fits = (
            sizes.blocks + 1 <= CODE
            and sizes.rows & (sizes.rows - 1) == 0
            and (sizes.cols, sizes.reps, sizes.slots, sizes.pairs) == (2, 2, 8, 32)
            and density.shape[1:] == (64, 64)
        )
        if fits:
            return whole_form(sizes, density, left_index, right_index, pair_count)
        return panel_form(density, left_index, right_index, pair_count)

    in_specs = (
        P(("groups", "row", "col", "rep"), None, None),
        P(None, None, ("groups", "row", "col", "rep"), None),
        P(None, None, ("groups", "row", "col", "rep"), None),
        P(None, None, ("groups", "row", "col", "rep")),
    )
    out_specs = P(("groups", "row", "col", "rep"), None, None)
    return jax.shard_map(local, mesh=mesh, in_specs=in_specs, out_specs=out_specs, check_vma=False)
```

profile of v0, /device:TPU:0, one launch (start us, length us, event | category | flops | bytes accessed | tf_op | source)
XLA Modules:
  0.0 73.9 jit_solution(14424218620216330655)
XLA Ops:
  0.0 0.0 copy-start
  0.0 0.9 %copy-done = f32[8,64,64]{2,1,0:T(8,128)S(1)} copy-done((f32[8,64,64]{2,1,0:T(8,128)S(1)}, f32[8,64,64]{2,1,0:T(8,128)}, u32[]{:S(2)}) %copy-start) | copy-done | bytes 131096
  1.0 0.0 copy-start.1
  1.0 0.7 copy-done.1
  1.7 0.0 copy-start.2
  1.7 0.7 copy-done.2
  2.4 0.7 copy-done.3
  3.1 0.8 %shard_map.46.refs_0_ = f32[264,128]{1,0:T(8,128)S(1)} custom-call(f32[8,64,64]{2,1,0:T(8,128)S(1)} %copy-done, s32[2,2,8,32]{3,2,1,0:T(8,128)S(1)} %copy-done.1, s32[2,2,8,32]{3,2,1,0:T(8,128)S(1)} %copy-done.2, s32[2,2,8]{2,1,0:T(2,128)S(1)} %copy-done.3), custom_call_target="tpu_custom_call" | custom-call | tf_op jit(solution)/shard_map/pallas_call | solution.py:307
  3.9 0.5 collective-permute-start.7
  4.4 4.7 %collective-permute-start.5 = (f32[264,128]{1,0:T(8,128)S(1)}, f32[264,128]{1,0:T(8,128)S(1)}, u32[]{:S(2)}, u32[]{:S(2)}) collective-permute-start(f32[264,128]{1,0:T(8,128)S(1)} %shard_map.46.refs_0_), channel_id=1, source_target_pairs={{0,12},{4,8},{8,4},{12,0},{1,13},{5,9},{9,5},{13,1},{2,14},{6,10},... | collective-permute-start | bytes 405512 | tf_op jit(solution)/shard_map/ppermute | solution.py:323
  9.1 0.0 collective-permute-start.3
  9.1 1.7 %collective-permute-start.2 = (f32[264,128]{1,0:T(8,128)S(1)}, f32[264,128]{1,0:T(8,128)S(1)}, u32[]{:S(2)}, u32[]{:S(2)}) collective-permute-start(f32[264,128]{1,0:T(8,128)S(1)} %shard_map.46.refs_0_), channel_id=1, source_target_pairs={{0,6},{2,4},{4,2},{6,0},{8,14},{10,12},{12,10},{14,8},{1,7},{3,5},... | collective-permute-start | bytes 405512 | tf_op jit(solution)/shard_map/ppermute | solution.py:327
  10.8 1.2 %collective-permute-start.1 = (f32[264,128]{1,0:T(8,128)S(1)}, f32[264,128]{1,0:T(8,128)S(1)}, u32[]{:S(2)}, u32[]{:S(2)}) collective-permute-start(f32[264,128]{1,0:T(8,128)S(1)} %shard_map.46.refs_0_), channel_id=1, source_target_pairs={{0,4},{4,0},{8,12},{12,8},{1,5},{5,1},{9,13},{13,9},{2,6},{6,2},{1... | collective-permute-start | bytes 405512 | tf_op jit(solution)/shard_map/ppermute | solution.py:323
  12.1 0.0 collective-permute-done.7.refs_8_
  12.1 0.5 collective-permute-start
  12.6 1.0 %collective-permute-done.5.refs_6_ = f32[264,128]{1,0:T(8,128)S(1)} collective-permute-done((f32[264,128]{1,0:T(8,128)S(1)}, f32[264,128]{1,0:T(8,128)S(1)}, u32[]{:S(2)}, u32[]{:S(2)}) %collective-permute-start.5) | collective-permute-done | bytes 135200 | tf_op jit(solution)/shard_map/ppermute | solution.py:323
  13.7 0.0 collective-permute-start.13
  13.7 7.6 %collective-permute-done.3.refs_4_ = f32[264,128]{1,0:T(8,128)S(1)} collective-permute-done((f32[264,128]{1,0:T(8,128)S(1)}, f32[264,128]{1,0:T(8,128)S(1)}, u32[]{:S(2)}, u32[]{:S(2)}) %collective-permute-start.3) | collective-permute-done | bytes 135200 | tf_op jit(solution)/shard_map/ppermute | solution.py:323
  21.3 1.5 %collective-permute-start.6 = (f32[264,128]{1,0:T(8,128)S(1)}, f32[264,128]{1,0:T(8,128)S(1)}, u32[]{:S(2)}, u32[]{:S(2)}) collective-permute-start(f32[264,128]{1,0:T(8,128)S(1)} %collective-permute-done.5.refs_6_), channel_id=1, source_target_pairs={{0,2},{2,0},{1,3},{3,1},{4,6},{6,4},{5,7},{7,5},{8,10},{10,8},{9,1... | collective-permute-start | bytes 405512 | tf_op jit(solution)/shard_map/ppermute | solution.py:330
  22.8 0.0 collective-permute-done.2.refs_3_
  22.8 0.0 collective-permute-start.11
  22.8 0.0 collective-permute-done.1.refs_2_
  22.8 0.9 %collective-permute-start.4 = (f32[264,128]{1,0:T(8,128)S(1)}, f32[264,128]{1,0:T(8,128)S(1)}, u32[]{:S(2)}, u32[]{:S(2)}) collective-permute-start(f32[264,128]{1,0:T(8,128)S(1)} %collective-permute-done.3.refs_4_), channel_id=1, source_target_pairs={{0,2},{2,0},{1,3},{3,1},{4,6},{6,4},{5,7},{7,5},{8,10},{10,8},{9,1... | collective-permute-start | bytes 405512 | tf_op jit(solution)/shard_map/ppermute | solution.py:330
  23.6 0.0 collective-permute-done.refs_1_
  23.6 0.0 collective-permute-start.10
  23.6 0.0 collective-permute-done.13.refs_14_
  23.6 0.5 collective-permute-start.9
  24.1 2.7 %collective-permute-done.6.refs_7_ = f32[264,128]{1,0:T(8,128)S(1)} collective-permute-done((f32[264,128]{1,0:T(8,128)S(1)}, f32[264,128]{1,0:T(8,128)S(1)}, u32[]{:S(2)}, u32[]{:S(2)}) %collective-permute-start.6) | collective-permute-done | bytes 135200 | tf_op jit(solution)/shard_map/ppermute | solution.py:330
  26.8 0.0 collective-permute-start.8
  26.8 0.0 collective-permute-done.11.refs_12_
  26.8 0.5 collective-permute-start.14
  27.3 1.9 %collective-permute-done.4.refs_5_ = f32[264,128]{1,0:T(8,128)S(1)} collective-permute-done((f32[264,128]{1,0:T(8,128)S(1)}, f32[264,128]{1,0:T(8,128)S(1)}, u32[]{:S(2)}, u32[]{:S(2)}) %collective-permute-start.4) | collective-permute-done | bytes 135200 | tf_op jit(solution)/shard_map/ppermute | solution.py:330
  29.3 0.0 collective-permute-start.12
  29.3 0.0 collective-permute-done.10.refs_11_
  29.3 0.0 collective-permute-done.9.refs_10_
  29.3 0.0 collective-permute-done.8.refs_9_
  29.3 0.0 collective-permute-done.14.refs_15_
  29.3 1.3 %collective-permute-done.12.refs_13_ = f32[264,128]{1,0:T(8,128)S(1)} collective-permute-done((f32[264,128]{1,0:T(8,128)S(1)}, f32[264,128]{1,0:T(8,128)S(1)}, u32[]{:S(2)}, u32[]{:S(2)}) %collective-permute-start.12) | collective-permute-done | bytes 135200 | tf_op jit(solution)/shard_map/ppermute | solution.py:333
  30.6 14.9 %shard_map.47 = (f32[64,32,128]{2,1,0:T(8,128)S(1)}, bf16[129,64,128]{2,1,0:T(8,128)(2,1)S(1)}, s32[128,128]{1,0:T(8,128)S(1)}) custom-call(f32[264,128]{1,0:T(8,128)S(1)} %shard_map.46.refs_0_, f32[264,128]{1,0:T(8,128)S(1)} %collective-permute-done.refs_1_, f32[264,128]{1,0:T(8,128)S(1)} %collective-permute-done.1.refs_2_, ...), custom_call_target="tpu_custom_call" | custom-call | tf_op jit(solution)/shard_map/pallas_call | solution.py:341
  45.5 0.2 collective-permute-start.15
  45.7 2.5 %collective-permute-done.15.other = f32[64,32,128]{2,1,0:T(8,128)S(1)} collective-permute-done((f32[64,32,128]{2,1,0:T(8,128)S(1)}, f32[64,32,128]{2,1,0:T(8,128)S(1)}, u32[]{:S(2)}, u32[]{:S(2)}) %collective-permute-start.15) | collective-permute-done | bytes 1048608 | tf_op jit(solution)/shard_map/ppermute | solution.py:333
  48.3 12.7 %shard_map.48.own = f32[64,32,128]{2,1,0:T(8,128)S(1)} custom-call(f32[64,32,128]{2,1,0:T(8,128)S(1)} %get-tuple-element.10.own, f32[64,32,128]{2,1,0:T(8,128)S(1)} %collective-permute-done.15.other, bf16[129,64,128]{2,1,0:T(8,128)(2,1)S(1)} %get-tuple-element.11.right_ref, s32[128,128]{1,0:T(8,128)S(1)} %get-tuple-element.12.codes_in), custom_call_target="tpu_custom_call" | custom-call | tf_op jit(solution)/shard_map/pallas_call | solution.py:349
  60.9 0.2 collective-permute-start.16
  61.1 2.5 %collective-permute-done.16.other = f32[64,32,128]{2,1,0:T(8,128)S(1)} collective-permute-done((f32[64,32,128]{2,1,0:T(8,128)S(1)}, f32[64,32,128]{2,1,0:T(8,128)S(1)}, u32[]{:S(2)}, u32[]{:S(2)}) %collective-permute-start.16) | collective-permute-done | bytes 1048608 | tf_op jit(solution)/shard_map/ppermute | solution.py:333
  63.7 4.7 %shard_map.49 = (f32[16,32,128]{2,1,0:T(8,128)S(1)}, bf16[129,64,128]{2,1,0:T(8,128)(2,1)S(1)}) custom-call(f32[64,32,128]{2,1,0:T(8,128)S(1)} %shard_map.48.own, f32[64,32,128]{2,1,0:T(8,128)S(1)} %collective-permute-done.16.other, s32[128,128]{1,0:T(8,128)S(1)} %get-tuple-element.12.codes_in), custom_call_target="tpu_custom_call" | custom-call | tf_op jit(solution)/shard_map/pallas_call | solution.py:357
  68.3 0.2 collective-permute-start.17
  68.5 1.4 %collective-permute-done.17.other = f32[16,32,128]{2,1,0:T(8,128)S(1)} collective-permute-done((f32[16,32,128]{2,1,0:T(8,128)S(1)}, f32[16,32,128]{2,1,0:T(8,128)S(1)}, u32[]{:S(2)}, u32[]{:S(2)}) %collective-permute-start.17) | collective-permute-done | bytes 262176 | tf_op jit(solution)/shard_map/ppermute | solution.py:333
  69.9 4.0 %shard_map.50 = f32[8,64,64]{2,1,0:T(8,128)} custom-call(f32[16,32,128]{2,1,0:T(8,128)S(1)} %get-tuple-element.13.own, f32[16,32,128]{2,1,0:T(8,128)S(1)} %collective-permute-done.17.other, bf16[129,64,128]{2,1,0:T(8,128)(2,1)S(1)} %get-tuple-element.14.right_ref, s32[128,128]{1,0:T(8,128)S(1)} %get-tuple-element.12.codes_in), custom_call_target="tpu_custom_call" | custom-call | tf_op jit(solution)/shard_map/pallas_call | solution.py:365
  (1 shorter events, 0.0 us)
Async XLA Ops:
  0.0 0.9 %copy-start = (f32[8,64,64]{2,1,0:T(8,128)S(1)}, f32[8,64,64]{2,1,0:T(8,128)}, u32[]{:S(2)}) copy-start(f32[8,64,64]{2,1,0:T(8,128)} %density.1) | copy-start | bytes 393220
  1.0 0.7 copy-start.1
  1.7 0.7 copy-start.2
  2.4 0.7 copy-start.3
  3.9 8.2 %collective-permute-start.7 = (f32[264,128]{1,0:T(8,128)S(1)}, f32[264,128]{1,0:T(8,128)S(1)}, u32[]{:S(2)}, u32[]{:S(2)}) collective-permute-start(f32[264,128]{1,0:T(8,128)S(1)} %shard_map.46.refs_0_), channel_id=1, source_target_pairs={{0,1},{1,0},{2,3},{3,2},{4,5},{5,4},{6,7},{7,6},{8,9},{9,8},{10,11... | collective-permute-start | bytes 405512 | tf_op jit(solution)/shard_map/ppermute | solution.py:333
  4.4 9.2 %collective-permute-start.5 = (f32[264,128]{1,0:T(8,128)S(1)}, f32[264,128]{1,0:T(8,128)S(1)}, u32[]{:S(2)}, u32[]{:S(2)}) collective-permute-start(f32[264,128]{1,0:T(8,128)S(1)} %shard_map.46.refs_0_), channel_id=1, source_target_pairs={{0,12},{4,8},{8,4},{12,0},{1,13},{5,9},{9,5},{13,1},{2,14},{6,10},... | collective-permute-start | bytes 405512 | tf_op jit(solution)/shard_map/ppermute | solution.py:323
  9.1 12.1 %collective-permute-start.3 = (f32[264,128]{1,0:T(8,128)S(1)}, f32[264,128]{1,0:T(8,128)S(1)}, u32[]{:S(2)}, u32[]{:S(2)}) collective-permute-start(f32[264,128]{1,0:T(8,128)S(1)} %shard_map.46.refs_0_), channel_id=1, source_target_pairs={{0,8},{4,12},{8,0},{12,4},{1,9},{5,13},{9,1},{13,5},{2,10},{6,14},... | collective-permute-start | bytes 405512 | tf_op jit(solution)/shard_map/ppermute | solution.py:323
  9.1 13.6 %collective-permute-start.2 = (f32[264,128]{1,0:T(8,128)S(1)}, f32[264,128]{1,0:T(8,128)S(1)}, u32[]{:S(2)}, u32[]{:S(2)}) collective-permute-start(f32[264,128]{1,0:T(8,128)S(1)} %shard_map.46.refs_0_), channel_id=1, source_target_pairs={{0,6},{2,4},{4,2},{6,0},{8,14},{10,12},{12,10},{14,8},{1,7},{3,5},... | collective-permute-start | bytes 405512 | tf_op jit(solution)/shard_map/ppermute | solution.py:327
  10.8 11.9 %collective-permute-start.1 = (f32[264,128]{1,0:T(8,128)S(1)}, f32[264,128]{1,0:T(8,128)S(1)}, u32[]{:S(2)}, u32[]{:S(2)}) collective-permute-start(f32[264,128]{1,0:T(8,128)S(1)} %shard_map.46.refs_0_), channel_id=1, source_target_pairs={{0,4},{4,0},{8,12},{12,8},{1,5},{5,1},{9,13},{13,9},{2,6},{6,2},{1... | collective-permute-start | bytes 405512 | tf_op jit(solution)/shard_map/ppermute | solution.py:323
  12.1 11.5 %collective-permute-start = (f32[264,128]{1,0:T(8,128)S(1)}, f32[264,128]{1,0:T(8,128)S(1)}, u32[]{:S(2)}, u32[]{:S(2)}) collective-permute-start(f32[264,128]{1,0:T(8,128)S(1)} %shard_map.46.refs_0_), channel_id=1, source_target_pairs={{0,2},{2,0},{1,3},{3,1},{4,6},{6,4},{5,7},{7,5},{8,10},{10,8},{9,1... | collective-permute-start | bytes 405512 | tf_op jit(solution)/shard_map/ppermute | solution.py:330
  13.7 10.0 %collective-permute-start.13 = (f32[264,128]{1,0:T(8,128)S(1)}, f32[264,128]{1,0:T(8,128)S(1)}, u32[]{:S(2)}, u32[]{:S(2)}) collective-permute-start(f32[264,128]{1,0:T(8,128)S(1)} %collective-permute-done.5.refs_6_), channel_id=1, source_target_pairs={{0,1},{1,0},{2,3},{3,2},{4,5},{5,4},{6,7},{7,6},{8,9},{9,8},{10,11... | collective-permute-start | bytes 405512 | tf_op jit(solution)/shard_map/ppermute | solution.py:333
  21.3 5.6 %collective-permute-start.6 = (f32[264,128]{1,0:T(8,128)S(1)}, f32[264,128]{1,0:T(8,128)S(1)}, u32[]{:S(2)}, u32[]{:S(2)}) collective-permute-start(f32[264,128]{1,0:T(8,128)S(1)} %collective-permute-done.5.refs_6_), channel_id=1, source_target_pairs={{0,2},{2,0},{1,3},{3,1},{4,6},{6,4},{5,7},{7,5},{8,10},{10,8},{9,1... | collective-permute-start | bytes 405512 | tf_op jit(solution)/shard_map/ppermute | solution.py:330
  22.8 4.1 %collective-permute-start.11 = (f32[264,128]{1,0:T(8,128)S(1)}, f32[264,128]{1,0:T(8,128)S(1)}, u32[]{:S(2)}, u32[]{:S(2)}) collective-permute-start(f32[264,128]{1,0:T(8,128)S(1)} %collective-permute-done.3.refs_4_), channel_id=1, source_target_pairs={{0,1},{1,0},{2,3},{3,2},{4,5},{5,4},{6,7},{7,6},{8,9},{9,8},{10,11... | collective-permute-start | bytes 405512 | tf_op jit(solution)/shard_map/ppermute | solution.py:333
  22.8 6.5 %collective-permute-start.4 = (f32[264,128]{1,0:T(8,128)S(1)}, f32[264,128]{1,0:T(8,128)S(1)}, u32[]{:S(2)}, u32[]{:S(2)}) collective-permute-start(f32[264,128]{1,0:T(8,128)S(1)} %collective-permute-done.3.refs_4_), channel_id=1, source_target_pairs={{0,2},{2,0},{1,3},{3,1},{4,6},{6,4},{5,7},{7,5},{8,10},{10,8},{9,1... | collective-permute-start | bytes 405512 | tf_op jit(solution)/shard_map/ppermute | solution.py:330
  23.6 5.6 %collective-permute-start.10 = (f32[264,128]{1,0:T(8,128)S(1)}, f32[264,128]{1,0:T(8,128)S(1)}, u32[]{:S(2)}, u32[]{:S(2)}) collective-permute-start(f32[264,128]{1,0:T(8,128)S(1)} %collective-permute-done.2.refs_3_), channel_id=1, source_target_pairs={{0,1},{1,0},{2,3},{3,2},{4,5},{5,4},{6,7},{7,6},{8,9},{9,8},{10,11... | collective-permute-start | bytes 405512 | tf_op jit(solution)/shard_map/ppermute | solution.py:333
  23.6 5.6 %collective-permute-start.9 = (f32[264,128]{1,0:T(8,128)S(1)}, f32[264,128]{1,0:T(8,128)S(1)}, u32[]{:S(2)}, u32[]{:S(2)}) collective-permute-start(f32[264,128]{1,0:T(8,128)S(1)} %collective-permute-done.1.refs_2_), channel_id=1, source_target_pairs={{0,1},{1,0},{2,3},{3,2},{4,5},{5,4},{6,7},{7,6},{8,9},{9,8},{10,11... | collective-permute-start | bytes 405512 | tf_op jit(solution)/shard_map/ppermute | solution.py:333
  26.8 2.4 %collective-permute-start.8 = (f32[264,128]{1,0:T(8,128)S(1)}, f32[264,128]{1,0:T(8,128)S(1)}, u32[]{:S(2)}, u32[]{:S(2)}) collective-permute-start(f32[264,128]{1,0:T(8,128)S(1)} %collective-permute-done.refs_1_), channel_id=1, source_target_pairs={{0,1},{1,0},{2,3},{3,2},{4,5},{5,4},{6,7},{7,6},{8,9},{9,8},{10,11... | collective-permute-start | bytes 405512 | tf_op jit(solution)/shard_map/ppermute | solution.py:333
  26.8 2.4 %collective-permute-start.14 = (f32[264,128]{1,0:T(8,128)S(1)}, f32[264,128]{1,0:T(8,128)S(1)}, u32[]{:S(2)}, u32[]{:S(2)}) collective-permute-start(f32[264,128]{1,0:T(8,128)S(1)} %collective-permute-done.6.refs_7_), channel_id=1, source_target_pairs={{0,1},{1,0},{2,3},{3,2},{4,5},{5,4},{6,7},{7,6},{8,9},{9,8},{10,11... | collective-permute-start | bytes 405512 | tf_op jit(solution)/shard_map/ppermute | solution.py:333
  29.3 1.4 %collective-permute-start.12 = (f32[264,128]{1,0:T(8,128)S(1)}, f32[264,128]{1,0:T(8,128)S(1)}, u32[]{:S(2)}, u32[]{:S(2)}) collective-permute-start(f32[264,128]{1,0:T(8,128)S(1)} %collective-permute-done.4.refs_5_), channel_id=1, source_target_pairs={{0,1},{1,0},{2,3},{3,2},{4,5},{5,4},{6,7},{7,6},{8,9},{9,8},{10,11... | collective-permute-start | bytes 405512 | tf_op jit(solution)/shard_map/ppermute | solution.py:333
  45.5 2.7 %collective-permute-start.15 = (f32[64,32,128]{2,1,0:T(8,128)S(1)}, f32[64,32,128]{2,1,0:T(8,128)S(1)}, u32[]{:S(2)}, u32[]{:S(2)}) collective-permute-start(f32[64,32,128]{2,1,0:T(8,128)S(1)} %get-tuple-element.10.own), channel_id=1, source_target_pairs={{0,1},{1,0},{2,3},{3,2},{4,5},{5,4},{6,7},{7,6},{8,9},{9,8},{10,11... | collective-permute-start | bytes 3145736 | tf_op jit(solution)/shard_map/ppermute | solution.py:333
  60.9 2.7 %collective-permute-start.16 = (f32[64,32,128]{2,1,0:T(8,128)S(1)}, f32[64,32,128]{2,1,0:T(8,128)S(1)}, u32[]{:S(2)}, u32[]{:S(2)}) collective-permute-start(f32[64,32,128]{2,1,0:T(8,128)S(1)} %shard_map.48.own), channel_id=1, source_target_pairs={{0,1},{1,0},{2,3},{3,2},{4,5},{5,4},{6,7},{7,6},{8,9},{9,8},{10,11... | collective-permute-start | bytes 3145736 | tf_op jit(solution)/shard_map/ppermute | solution.py:333
  68.3 1.6 %collective-permute-start.17 = (f32[16,32,128]{2,1,0:T(8,128)S(1)}, f32[16,32,128]{2,1,0:T(8,128)S(1)}, u32[]{:S(2)}, u32[]{:S(2)}) collective-permute-start(f32[16,32,128]{2,1,0:T(8,128)S(1)} %get-tuple-element.13.own), channel_id=1, source_target_pairs={{0,1},{1,0},{2,3},{3,2},{4,5},{5,4},{6,7},{7,6},{8,9},{9,8},{10,11... | collective-permute-start | bytes 786440 | tf_op jit(solution)/shard_map/ppermute | solution.py:333
where the time goes:
time: 74.3 us; the launch traced here: 73.9 us
  Pallas kernels  37.1 us (50%)
  waiting for transfers between devices  21 us (28%)
  starting transfers between devices  12.7 us (17%)
  local copies, waits for them, and re-layouts  3.06 us (4%)
    pallas_call x1, Pallas kernels, whole_form(): call(first_square_kernel, sizes, [packed(sizes.half), rights, jax.ShapeDt...  14.9 us
    pallas_call x1, Pallas kernels, whole_form(): call(first_cube_kernel, sizes, packed(sizes.half), [VMEM] * 3 + [ANY], VM...  12.7 us
    ppermute x3, waiting for transfers between devices, row_swap(): return lax.ppermute(value, 'row', [(i, i ^ m) for i in range(sizes.rows)])  8.65 us
    ppermute x11, waiting for transfers between devices, rep_swap(): return lax.ppermute(value, 'rep', [(0, 1), (1, 0)])  7.78 us
    ppermute x3, starting transfers between devices, row_swap(): return lax.ppermute(value, 'row', [(i, i ^ m) for i in range(sizes.rows)])  5.92 us
    pallas_call x1, Pallas kernels, whole_form(): call(last_square_kernel, sizes, [packed(sizes.cols * sizes.slots), rights...  4.65 us
    ppermute x3, waiting for transfers between devices, col_swap(): return lax.ppermute(value, 'col', [(0, 1), (1, 0)])  4.6 us
    pallas_call x1, Pallas kernels, whole_form(): call(last_cube_kernel, sizes, jax.ShapeDtypeStruct(density.shape, F32), [...  3.97 us
  transfers between devices with their start and end apart: 18, of which 8 were waited for; matrix products, arithmetic and copies ran while one was open for 0% of the time, Pallas kernels for 0%

commit v1 on v0

--- a/solution.py
+++ b/solution.py
@@ -113,7 +113,7 @@
         right_ref[right_at] = jnp.zeros((64, 128), BF16)
 
 
-def filtered(codes, at, lane, pairs, left_ref, right_ref):
+def block_products(codes, at, lane, pairs, left_ref, right_ref):
     mask = left_lanes(128)
     total = jnp.zeros((128, 128), F32)
     for start in range(0, pairs, CHUNK):
@@ -127,8 +127,40 @@
         )
         right = jnp.concatenate(rights, axis=0)
         total = total + jnp.dot(left, right, preferred_element_type=F32)
+    return total
+
+
+def fold(total):
     both = total[:64] + total[64:]
     return both + pltpu.roll(both, 64, 1)
+
+
+def ordered_products(sizes, codes, line, first, product, blocks, group, left_ref, right_ref, finish):
+    lane = product * sizes.pairs
+    limits = (0, sizes.pairs // 2, 3 * sizes.pairs // 4, sizes.pairs)
+
+    def body(g, carry):
+        most = codes[line + product, g * group] >> 8
+        for low, high in zip(limits[:-1], limits[1:]):
+
+            @pl.when((most > low) & (most <= high))
+            def _():
+                for s in range(group):
+                    place = (codes[line + product, g * group + s] & (CODE - 1)) - first
+                    finish(place, fold(block_products(codes, place, lane, high, left_ref, right_ref)))
+
+        return carry
+
+    lax.fori_loop(0, blocks // group, body, 0)
+
+
+def order_by_count(codes, lane, wanted, blocks):
+    block = lax.broadcasted_iota(jnp.int32, (blocks, 128), 0)
+    count = jnp.broadcast_to(codes[:, lane : lane + 1] >> 16, (blocks, 128))
+    key = jnp.where(wanted(block), count * CODE + block, -1 - block).astype(F32)
+    rank = jnp.sum((key.T > key).astype(F32), axis=1, keepdims=True).astype(jnp.int32)
+    place = lax.broadcasted_iota(jnp.int32, (blocks, 128), 1)
+    return jnp.sum(jnp.where(rank == place, key, 0.0), axis=0, keepdims=True).astype(jnp.int32)
 
 
 class Sizes:
@@ -140,6 +172,7 @@
         self.tiles = self.rows * self.cols
         self.blocks = self.tiles * self.tile
         self.half = self.tiles * slots
+        self.strip = self.cols * slots
 
 
 def pack_kernel(sizes, density, left_index, right_index, pair_count, out, blocks, lefts, rights, counts, sems):
@@ -176,39 +209,52 @@
         out[s * 32 : s * 32 + 32] = jnp.concatenate([blocks[s, :32], blocks[s, 32:]], axis=1)
 
 
-def first_square_kernel(sizes, *refs):
-    count = sizes.tiles * sizes.reps
-    pieces, (out, right_ref, codes_out, left_ref, codes, sem) = refs[:count], refs[count:]
+def first_square_kernel(sizes, offsets, *refs):
+    pieces, refs = refs[: len(offsets)], refs[len(offsets) :]
+    out, right_ref, codes_out, left_ref, codes, sem, payload, payload_sem = refs
     row, col, rep = lax.axis_index("row"), lax.axis_index("col"), lax.axis_index("rep")
-    places = []
-    for e in range(sizes.reps):
-        for m in range(sizes.rows):
-            for n in range(sizes.cols):
-                tile = (row ^ m) * sizes.cols + (col ^ n)
-                places.append(pl.multiple_of(tile * sizes.tile + (rep ^ e) * sizes.slots, sizes.slots))
-    for piece, base in zip(pieces, places):
-        codes_out[pl.ds(base, sizes.slots)] = piece[sizes.slots * 32 : sizes.slots * 33].astype(jnp.int32)
-    copy = pltpu.make_async_copy(codes_out, codes, sem)
-    copy.start()
-    zero_block(left_ref, sizes.blocks, right_ref, sizes.blocks)
-    for piece, base in zip(pieces, places):
+    fetch = pltpu.make_async_copy(pieces[-1], payload, payload_sem)
+    fetch.start()
+    pieces = pieces[:-1] + (payload,)
+
+    def unpack(piece, offset):
+        m, n, e = offset
+        tile = (row ^ m) * sizes.cols + (col ^ n)
+        base = pl.multiple_of(tile * sizes.tile + (rep ^ e) * sizes.slots, sizes.slots)
         for s in range(sizes.slots):
             twice = spread(piece[s * 32 : s * 32 + 32])
             store_left(left_ref, base + s, twice)
             store_right(right_ref, base + s, twice)
+
+    def unpack_codes(piece, offset):
+        m, n, e = offset
+        if e == 0:
+            place = pl.multiple_of(((row ^ m) * sizes.cols + (col ^ n)) * sizes.slots, sizes.slots)
+            codes_out[pl.ds(place, sizes.slots)] = piece[sizes.slots * 32 : sizes.slots * 33].astype(jnp.int32)
+
+    fetch.wait()
+    for piece, offset in zip(pieces, offsets):
+        unpack_codes(piece, offset)
+    mine = lambda place: place < sizes.half
+    wanted = (mine, mine, lambda place: mine(place) & (place // sizes.strip == row))
+    for product, choice in enumerate(wanted):
+        order = order_by_count(codes_out[: sizes.blocks], product * sizes.pairs, choice, sizes.blocks)
+        codes_out[sizes.half + product : sizes.half + product + 1] = order
+    copy = pltpu.make_async_copy(codes_out.at[pl.ds(0, sizes.half + 8)], codes, sem)
+    copy.start()
+    zero_block(left_ref, sizes.blocks, right_ref, sizes.blocks)
+    for piece, offset in zip(pieces, offsets):
+        unpack(piece, offset)
     copy.wait()
 
-    def body(i, carry):
-        base = (i * sizes.reps + rep) * sizes.slots
-        for s in range(sizes.slots):
-            out[i * sizes.slots + s] = pack(filtered(codes, base + s, 0, sizes.pairs, left_ref, right_ref))
-        return carry
-
-    lax.fori_loop(0, sizes.tiles, body, 0)
+    def finish(place, twice):
+        out[place] = pack(twice)
+
+    ordered_products(sizes, codes, sizes.half, 0, 0, sizes.half, 16, left_ref, right_ref, finish)
 
 
 def first_cube_kernel(sizes, own, other, right_ref, codes_in, out, left_ref, codes, sem):
-    copy = pltpu.make_async_copy(codes_in, codes, sem)
+    copy = pltpu.make_async_copy(codes_in.at[pl.ds(0, sizes.half + 8)], codes, sem)
     copy.start()
     rep = lax.axis_index("rep")
     zero_block(left_ref, sizes.blocks, None, None)
@@ -224,20 +270,21 @@
     lax.fori_loop(0, sizes.tiles, prepare_tile, 0)
     copy.wait()
 
-    def body(i, carry):
-        base = (i * sizes.reps + rep) * sizes.slots
-        for s in range(sizes.slots):
-            cube = pack(filtered(codes, base + s, sizes.pairs, sizes.pairs, left_ref, right_ref))
-            out[i * sizes.slots + s] = 3.0 * own[i * sizes.slots + s] - 2.0 * cube
-        return carry
-
-    lax.fori_loop(0, sizes.tiles, body, 0)
-
-
-def last_square_kernel(sizes, own, other, codes_in, out, right_ref, left_ref, codes, sem):
-    copy = pltpu.make_async_copy(codes_in, codes, sem)
-    copy.start()
+    def finish(place, twice):
+        out[place] = 3.0 * own[place] - 2.0 * pack(twice)
+
+    ordered_products(sizes, codes, sizes.half, 0, 1, sizes.half, 16, left_ref, right_ref, finish)
+
+
+def last_square_kernel(sizes, own, other, codes_in, out, right_ref, left_ref, codes, sems):
     row, rep = lax.axis_index("row"), lax.axis_index("rep")
+    first = pl.multiple_of(row * sizes.strip, sizes.strip)
+    copies = [
+        pltpu.make_async_copy(codes_in.at[pl.ds(first, sizes.strip)], codes.at[pl.ds(0, sizes.strip)], sems.at[0]),
+        pltpu.make_async_copy(codes_in.at[pl.ds(sizes.half, 8)], codes.at[pl.ds(sizes.strip, 8)], sems.at[1]),
+    ]
+    for copy in copies:
+        copy.start()
     zero_block(left_ref, sizes.panel, right_ref, sizes.blocks)
 
     def prepare_tile(i, carry):
@@ -254,23 +301,20 @@
             for s in range(sizes.slots):
                 twice = spread(source[(row * sizes.cols + n) * sizes.slots + s])
                 store_left(left_ref, (n * sizes.reps + e) * sizes.slots + s, twice)
-    copy.wait()
-
-    def body(n, carry):
-        base = row * sizes.panel + (n * sizes.reps + rep) * sizes.slots
-        for s in range(sizes.slots):
-            out[n * sizes.slots + s] = pack(
-                filtered(codes, base + s, 2 * sizes.pairs, sizes.pairs, left_ref, right_ref)
-            )
-        return carry
-
-    lax.fori_loop(0, sizes.cols, body, 0)
+    for copy in copies:
+        copy.wait()
+
+    def finish(place, twice):
+        out[place] = pack(twice)
+
+    ordered_products(sizes, codes, sizes.strip, first, 2, sizes.strip, 8, left_ref, right_ref, finish)
 
 
 def last_cube_kernel(sizes, own, other, right_ref, codes_in, out, left_ref, codes, sem):
-    copy = pltpu.make_async_copy(codes_in, codes, sem)
+    row, col, rep = lax.axis_index("row"), lax.axis_index("col"), lax.axis_index("rep")
+    base = pl.multiple_of((row * sizes.cols + col) * sizes.slots, sizes.slots)
+    copy = pltpu.make_async_copy(codes_in.at[pl.ds(base, sizes.slots)], codes, sem)
     copy.start()
-    row, col, rep = lax.axis_index("row"), lax.axis_index("col"), lax.axis_index("rep")
     zero_block(left_ref, sizes.panel, None, None)
     for n in range(sizes.cols):
         for e, source in ((rep, own), (1 - rep, other)):
@@ -278,9 +322,8 @@
                 twice = spread(source[n * sizes.slots + s])
                 store_left(left_ref, (n * sizes.reps + e) * sizes.slots + s, twice)
     copy.wait()
-    base = row * sizes.panel + (col * sizes.reps + rep) * sizes.slots
     for s in range(sizes.slots):
-        cube = filtered(codes, base + s, 3 * sizes.pairs, sizes.pairs, left_ref, right_ref)
+        cube = fold(block_products(codes, s, 3 * sizes.pairs, sizes.pairs, left_ref, right_ref))
         square = spread(own[col * sizes.slots + s])
         out[s] = (3.0 * square - 2.0 * cube)[:, :64]
 
@@ -299,10 +342,13 @@
 def whole_form(sizes, density, left_index, right_index, pair_count):
     width = density.shape[1]
     index_shape = (STEPS, 2, sizes.slots, sizes.pairs)
-    code_shape = (sizes.blocks, STEPS * 2 * sizes.pairs)
+    code_shape = (sizes.blocks + 8, STEPS * 2 * sizes.pairs)
     packed = lambda count: jax.ShapeDtypeStruct((count, 32, 128), F32)
     rights = jax.ShapeDtypeStruct((sizes.blocks + 1, 64, 128), BF16)
-    code_scratch = [pltpu.SMEM(code_shape, jnp.int32), pltpu.SemaphoreType.DMA]
+    code_scratch = [
+        pltpu.SMEM((sizes.half + 8, code_shape[1]), jnp.int32),
+        pltpu.SemaphoreType.DMA,
+    ]
 
     payload = call(
         pack_kernel,
@@ -317,34 +363,46 @@
             pltpu.SMEM((STEPS, 2, sizes.slots), jnp.int32),
             pltpu.SemaphoreType.DMA((4,)),
         ],
+        limit=62,
     )(density, left_index, right_index, pair_count)
 
+    def swap(value, axes, mask, size):
+        return lax.ppermute(value, axes, [(i, i ^ mask) for i in range(size)])
+
     def row_swap(value, m):
-        return lax.ppermute(value, "row", [(i, i ^ m) for i in range(sizes.rows)])
-
-    def both_swap(value, m):
-        axes = ("row", "col")
-        return lax.ppermute(value, axes, [(i, i ^ (2 * m + 1)) for i in range(2 * sizes.rows)])
+        return swap(value, "row", m, 4)
 
     def col_swap(value):
-        return lax.ppermute(value, "col", [(0, 1), (1, 0)])
+        return swap(value, "col", 1, 2)
 
     def rep_swap(value):
-        return lax.ppermute(value, "rep", [(0, 1), (1, 0)])
-
-    pieces = [payload, col_swap(payload)]
-    for m in range(1, sizes.rows):
-        arrived = row_swap(payload, m)
-        pieces += [arrived, both_swap(payload, m) if m == 1 else col_swap(arrived)]
-    pieces += [rep_swap(piece) for piece in pieces]
+        return swap(value, "rep", 1, 2)
+
+    far, near, across = row_swap(payload, 2), row_swap(payload, 1), col_swap(payload)
+    near_across, farthest = col_swap(near), row_swap(far, 1)
+    far_across, farthest_across = col_swap(far), swap(far, ("row", "col"), 3, 8)
+    own = [
+        ((0, 0, 0), swap(payload, "rep", 0, 2)),
+        ((1, 0, 0), near),
+        ((1, 1, 0), near_across),
+        ((0, 1, 0), across),
+        ((2, 0, 0), far),
+        ((3, 0, 0), farthest),
+        ((2, 1, 0), far_across),
+        ((3, 1, 0), farthest_across),
+    ]
+    pieces = [pair for (m, n, e), piece in own for pair in (((m, n, e), piece), ((m, n, 1), rep_swap(piece)))]
+    offsets, pieces = zip(*pieces[::-1])
 
     square, right, codes = call(
-        first_square_kernel,
+        lambda *args: first_square_kernel(args[0], offsets, *args[1:]),
         sizes,
         [packed(sizes.half), rights, jax.ShapeDtypeStruct(code_shape, jnp.int32)],
-        [VMEM] * len(pieces),
+        [VMEM] * (len(pieces) - 1) + [ANY],
         [VMEM] * 3,
-        [pltpu.VMEM((sizes.blocks + 1, 128, 128), BF16)] + code_scratch,
+        [pltpu.VMEM((sizes.blocks + 1, 128, 128), BF16)]
+        + code_scratch
+        + [pltpu.VMEM(payload.shape, F32), pltpu.SemaphoreType.DMA],
     )(*pieces)
     current = call(
         first_cube_kernel,
@@ -360,7 +418,11 @@
         [packed(sizes.cols * sizes.slots), rights],
         [VMEM] * 2 + [ANY],
         [VMEM] * 2,
-        [pltpu.VMEM((sizes.panel + 1, 128, 128), BF16)] + code_scratch,
+        [
+            pltpu.VMEM((sizes.panel + 1, 128, 128), BF16),
+            pltpu.SMEM((sizes.strip + 8, code_shape[1]), jnp.int32),
+            pltpu.SemaphoreType.DMA((2,)),
+        ],
     )(current, rep_swap(current), codes)
     return call(
         last_cube_kernel,
@@ -368,7 +430,11 @@
         jax.ShapeDtypeStruct(density.shape, F32),
         [VMEM] * 3 + [ANY],
         VMEM,
-        [pltpu.VMEM((sizes.panel + 1, 128, 128), BF16)] + code_scratch,
+        [
+            pltpu.VMEM((sizes.panel + 1, 128, 128), BF16),
+            pltpu.SMEM((sizes.slots, code_shape[1]), jnp.int32),
+            pltpu.SemaphoreType.DMA,
+        ],
     )(square, rep_swap(square), right, codes)
 
 
@@ -376,9 +442,7 @@
     def local(density, left_index, right_index, pair_count):
         sizes = Sizes(mesh.shape, density.shape[0], left_index.shape[3])
         fits = (
-            sizes.blocks + 1 <= CODE
-            and sizes.rows & (sizes.rows - 1) == 0
-            and (sizes.cols, sizes.reps, sizes.slots, sizes.pairs) == (2, 2, 8, 32)
+            (sizes.rows, sizes.cols, sizes.reps, sizes.slots, sizes.pairs) == (4, 2, 2, 8, 32)
             and density.shape[1:] == (64, 64)
         )
         if fits:

time: 74.3 us -> 61.8 us (0.83)
  waiting for transfers between devices: 21 us -> 13.3 us
  Pallas kernels: 37.1 us -> 30.5 us
  starting transfers between devices: 12.7 us -> 16.9 us
  local copies, waits for them, and re-layouts: 3.06 us -> 0 us
    ppermute x18 -> x19, waiting for transfers between devices: 21 us -> 13.3 us  [swap(): return lax.ppermute(value, axes, [(i, i ^ mask) for i in range(size)])]
    ppermute x18 -> x19, starting transfers between devices: 12.7 us -> 16.9 us  [swap(): return lax.ppermute(value, axes, [(i, i ^ mask) for i in range(size)])]
    pallas_call x1, Pallas kernels: 14.9 us -> 11.6 us  [whole_form(): call(lambda *args: first_square_kernel(args[0], offsets, *args[1:]), size...]
    unnamed x8 -> x0, local copies, waits for them, and re-layouts: 3.06 us -> none
    pallas_call x1, Pallas kernels: 12.7 us -> 10.2 us  [whole_form(): call(first_cube_kernel, sizes, packed(sizes.half), [VMEM] * 3 + [ANY], VM...]
    pallas_call x1, Pallas kernels: 3.97 us -> 2.84 us  [whole_form(): call(last_cube_kernel, sizes, jax.ShapeDtypeStruct(density.shape, F32), [...]
    pallas_call x1, Pallas kernels: 0.85 us -> 1.74 us  [whole_form(): call(pack_kernel, sizes, jax.ShapeDtypeStruct((sizes.slots * 33, 128), F3...]
  transfers between devices with their start and end apart: 18 -> 19, of which waited for: 8 -> 8; matrix products, arithmetic and copies ran while one was open for 0% -> 0% of each run, Pallas kernels for 0% -> 0%
where the time goes in v1:
time: 61.8 us; the launch traced here: 60.9 us
  Pallas kernels  30.5 us (49%)
  starting transfers between devices  16.9 us (27%)
  waiting for transfers between devices  13.3 us (22%)
    ppermute x19, starting transfers between devices, swap(): return lax.ppermute(value, axes, [(i, i ^ mask) for i in range(size)])  16.9 us
    ppermute x19, waiting for transfers between devices, swap(): return lax.ppermute(value, axes, [(i, i ^ mask) for i in range(size)])  13.3 us
    pallas_call x1, Pallas kernels, whole_form(): call(lambda *args: first_square_kernel(args[0], offsets, *args[1:]), size...  11.6 us
    pallas_call x1, Pallas kernels, whole_form(): call(first_cube_kernel, sizes, packed(sizes.half), [VMEM] * 3 + [ANY], VM...  10.2 us
    pallas_call x1, Pallas kernels, whole_form(): call(last_square_kernel, sizes, [packed(sizes.cols * sizes.slots), rights...  4.12 us
    pallas_call x1, Pallas kernels, whole_form(): call(last_cube_kernel, sizes, jax.ShapeDtypeStruct(density.shape, F32), [...  2.84 us
    pallas_call x1, Pallas kernels, whole_form(): call(pack_kernel, sizes, jax.ShapeDtypeStruct((sizes.slots * 33, 128), F3...  1.74 us
  transfers between devices with their start and end apart: 19, of which 8 were waited for; matrix products, arithmetic and copies ran while one was open for 0% of the time, Pallas kernels for 0%

profile of v1, /device:TPU:0, one launch (start us, length us, event | category | flops | bytes accessed | tf_op | source)
XLA Modules:
  0.0 60.9 jit_solution(15730873255025549006)
XLA Ops:
  0.0 1.7 %shard_map.46 = f32[264,128]{1,0:T(8,128)} custom-call(f32[8,64,64]{2,1,0:T(8,128)} %density.1, s32[2,2,8,32]{3,2,1,0:T(8,128)} %left_index.1, s32[2,2,8,32]{3,2,1,0:T(8,128)} %right_index.1, s32[2,2,8]{2,1,0:T(2,128)} %pair_count.1), custom_call_target="tpu_custom_call" | custom-call | tf_op jit(solution)/shard_map/pallas_call | solution.py:353
  1.7 0.9 %collective-permute-start.14 = (f32[264,128]{1,0:T(8,128)}, f32[264,128]{1,0:T(8,128)S(1)}, u32[]{:S(2)}, u32[]{:S(2)}) collective-permute-start(f32[264,128]{1,0:T(8,128)} %shard_map.46), channel_id=1, source_target_pairs={{0,0},{1,1},{2,2},{3,3},{4,4},{5,5},{6,6},{7,7},{8,8},{9,9},{10,10... | collective-permute-start | bytes 405512 | tf_op jit(solution)/shard_map/ppermute | solution.py:370
  2.7 3.0 %collective-permute-start.10 = (f32[264,128]{1,0:T(8,128)}, f32[264,128]{1,0:T(8,128)S(1)}, u32[]{:S(2)}, u32[]{:S(2)}) collective-permute-start(f32[264,128]{1,0:T(8,128)} %shard_map.46), channel_id=1, source_target_pairs={{0,4},{4,0},{8,12},{12,8},{1,5},{5,1},{9,13},{13,9},{2,6},{6,2},{1... | collective-permute-start | bytes 405512 | tf_op jit(solution)/shard_map/ppermute | solution.py:370
  5.7 1.5 %collective-permute-start.8 = (f32[264,128]{1,0:T(8,128)}, f32[264,128]{1,0:T(8,128)S(1)}, u32[]{:S(2)}, u32[]{:S(2)}) collective-permute-start(f32[264,128]{1,0:T(8,128)} %shard_map.46), channel_id=1, source_target_pairs={{0,2},{2,0},{1,3},{3,1},{4,6},{6,4},{5,7},{7,5},{8,10},{10,8},{9,1... | collective-permute-start | bytes 405512 | tf_op jit(solution)/shard_map/ppermute | solution.py:370
  7.2 2.6 %collective-permute-start = (f32[264,128]{1,0:T(8,128)}, f32[264,128]{1,0:T(8,128)S(1)}, u32[]{:S(2)}, u32[]{:S(2)}) collective-permute-start(f32[264,128]{1,0:T(8,128)} %shard_map.46), channel_id=1, source_target_pairs={{0,8},{4,12},{8,0},{12,4},{1,9},{5,13},{9,1},{13,5},{2,10},{6,14},... | collective-permute-start | bytes 405512 | tf_op jit(solution)/shard_map/ppermute | solution.py:370
  9.8 0.0 collective-permute-done.14.args_15_
  9.8 0.0 collective-permute-start.15
  9.8 0.0 collective-permute-done.10.args_13_
  9.8 0.5 collective-permute-start.13
  10.3 2.5 %collective-permute-start.11 = (f32[264,128]{1,0:T(8,128)S(1)}, f32[264,128]{1,0:T(8,128)S(1)}, u32[]{:S(2)}, u32[]{:S(2)}) collective-permute-start(f32[264,128]{1,0:T(8,128)S(1)} %collective-permute-done.10.args_13_), channel_id=1, source_target_pairs={{0,2},{2,0},{1,3},{3,1},{4,6},{6,4},{5,7},{7,5},{8,10},{10,8},{9,1... | collective-permute-start | bytes 405512 | tf_op jit(solution)/shard_map/ppermute | solution.py:370
  12.8 0.0 collective-permute-done.8.args_9_
  12.8 0.2 collective-permute-start.9
  13.0 3.0 %collective-permute-done.args_7_ = f32[264,128]{1,0:T(8,128)S(1)} collective-permute-done((f32[264,128]{1,0:T(8,128)}, f32[264,128]{1,0:T(8,128)S(1)}, u32[]{:S(2)}, u32[]{:S(2)}) %collective-permute-start) | collective-permute-done | bytes 135200 | tf_op jit(solution)/shard_map/ppermute | solution.py:370
  16.0 0.0 collective-permute-start.5
  16.0 0.0 collective-permute-done.15.args_14_
  16.0 0.8 %collective-permute-start.3 = (f32[264,128]{1,0:T(8,128)S(1)}, f32[264,128]{1,0:T(8,128)S(1)}, u32[]{:S(2)}, u32[]{:S(2)}) collective-permute-start(f32[264,128]{1,0:T(8,128)S(1)} %collective-permute-done.args_7_), channel_id=1, source_target_pairs={{0,2},{2,0},{1,3},{3,1},{4,6},{6,4},{5,7},{7,5},{8,10},{10,8},{9,1... | collective-permute-start | bytes 405512 | tf_op jit(solution)/shard_map/ppermute | solution.py:370
  16.7 0.0 collective-permute-done.13.args_12_
  16.7 2.7 %collective-permute-start.1 = (f32[264,128]{1,0:T(8,128)S(1)}, f32[264,128]{1,0:T(8,128)S(1)}, u32[]{:S(2)}, u32[]{:S(2)}) collective-permute-start(f32[264,128]{1,0:T(8,128)S(1)} %collective-permute-done.args_7_), channel_id=1, source_target_pairs={{0,6},{2,4},{4,2},{6,0},{8,14},{10,12},{12,10},{14,8},{1,7},{3,5},... | collective-permute-start | bytes 405512 | tf_op jit(solution)/shard_map/ppermute | solution.py:370
  19.5 0.0 collective-permute-done.11.args_11_
  19.5 0.0 collective-permute-start.7
  19.5 0.0 collective-permute-done.9.args_8_
  19.5 0.5 collective-permute-start.12
  20.0 2.0 %collective-permute-done.5.args_5_ = f32[264,128]{1,0:T(8,128)S(1)} collective-permute-done((f32[264,128]{1,0:T(8,128)S(1)}, f32[264,128]{1,0:T(8,128)S(1)}, u32[]{:S(2)}, u32[]{:S(2)}) %collective-permute-start.5) | collective-permute-done | bytes 135200 | tf_op jit(solution)/shard_map/ppermute | solution.py:370
  21.9 0.0 collective-permute-start.6
  21.9 1.5 %collective-permute-done.3.args_3_ = f32[264,128]{1,0:T(8,128)S(1)} collective-permute-done((f32[264,128]{1,0:T(8,128)S(1)}, f32[264,128]{1,0:T(8,128)S(1)}, u32[]{:S(2)}, u32[]{:S(2)}) %collective-permute-start.3) | collective-permute-done | bytes 135200 | tf_op jit(solution)/shard_map/ppermute | solution.py:370
  23.4 0.0 collective-permute-start.4
  23.4 0.0 collective-permute-done.1.args_1_
  23.4 0.5 collective-permute-start.2
  23.9 0.0 collective-permute-done.7.args_6_
  23.9 0.0 collective-permute-done.12.args_10_
  23.9 0.0 collective-permute-done.6.args_4_
  23.9 0.8 %collective-permute-done.4.args_2_ = f32[264,128]{1,0:T(8,128)S(1)} collective-permute-done((f32[264,128]{1,0:T(8,128)S(1)}, f32[264,128]{1,0:T(8,128)S(1)}, u32[]{:S(2)}, u32[]{:S(2)}) %collective-permute-start.4) | collective-permute-done | bytes 135200 | tf_op jit(solution)/shard_map/ppermute | solution.py:370
  24.7 0.2 collective-permute-done.2.args_0_
  24.9 11.6 %shard_map.47 = (f32[64,32,128]{2,1,0:T(8,128)S(1)}, bf16[129,64,128]{2,1,0:T(8,128)(2,1)S(1)}, s32[136,128]{1,0:T(8,128)S(1)}) custom-call(f32[264,128]{1,0:T(8,128)S(1)} %collective-permute-done.2.args_0_, f32[264,128]{1,0:T(8,128)S(1)} %collective-permute-done.1.args_1_, f32[264,128]{1,0:T(8,128)S(1)} %collective-permute-done.4.args_2_, ...), custom_call_target="tpu_custom_call" | custom-call | tf_op jit(solution)/shard_map/pallas_call | solution.py:397
  36.6 0.4 collective-permute-start.16
  36.9 2.3 %collective-permute-done.16.other = f32[64,32,128]{2,1,0:T(8,128)S(1)} collective-permute-done((f32[64,32,128]{2,1,0:T(8,128)S(1)}, f32[64,32,128]{2,1,0:T(8,128)S(1)}, u32[]{:S(2)}, u32[]{:S(2)}) %collective-permute-start.16) | collective-permute-done | bytes 1048608 | tf_op jit(solution)/shard_map/ppermute | solution.py:370
  39.3 10.2 %shard_map.48.own = f32[64,32,128]{2,1,0:T(8,128)S(1)} custom-call(f32[64,32,128]{2,1,0:T(8,128)S(1)} %get-tuple-element.10.own, f32[64,32,128]{2,1,0:T(8,128)S(1)} %collective-permute-done.16.other, bf16[129,64,128]{2,1,0:T(8,128)(2,1)S(1)} %get-tuple-element.11.right_ref, s32[136,128]{1,0:T(8,128)S(1)} %get-tuple-element.12.codes_in), custom_call_target="tpu_custom_call" | custom-call | tf_op jit(solution)/shard_map/pallas_call | solution.py:407
  49.5 0.4 collective-permute-start.17
  49.9 2.3 %collective-permute-done.17.other = f32[64,32,128]{2,1,0:T(8,128)S(1)} collective-permute-done((f32[64,32,128]{2,1,0:T(8,128)S(1)}, f32[64,32,128]{2,1,0:T(8,128)S(1)}, u32[]{:S(2)}, u32[]{:S(2)}) %collective-permute-start.17) | collective-permute-done | bytes 1048608 | tf_op jit(solution)/shard_map/ppermute | solution.py:370
  52.2 4.1 %shard_map.49 = (f32[16,32,128]{2,1,0:T(8,128)S(1)}, bf16[129,64,128]{2,1,0:T(8,128)(2,1)S(1)}) custom-call(f32[64,32,128]{2,1,0:T(8,128)S(1)} %shard_map.48.own, f32[64,32,128]{2,1,0:T(8,128)S(1)} %collective-permute-done.17.other, s32[136,128]{1,0:T(8,128)S(1)} %get-tuple-element.12.codes_in), custom_call_target="tpu_custom_call" | custom-call | tf_op jit(solution)/shard_map/pallas_call | solution.py:415
  56.3 0.4 collective-permute-start.18
  56.7 1.2 %collective-permute-done.18.other = f32[16,32,128]{2,1,0:T(8,128)S(1)} collective-permute-done((f32[16,32,128]{2,1,0:T(8,128)S(1)}, f32[16,32,128]{2,1,0:T(8,128)S(1)}, u32[]{:S(2)}, u32[]{:S(2)}) %collective-permute-start.18) | collective-permute-done | bytes 262176 | tf_op jit(solution)/shard_map/ppermute | solution.py:370
  57.9 2.8 %shard_map.50 = f32[8,64,64]{2,1,0:T(8,128)} custom-call(f32[16,32,128]{2,1,0:T(8,128)S(1)} %get-tuple-element.13.own, f32[16,32,128]{2,1,0:T(8,128)S(1)} %collective-permute-done.18.other, bf16[129,64,128]{2,1,0:T(8,128)(2,1)S(1)} %get-tuple-element.14.right_ref, s32[136,128]{1,0:T(8,128)S(1)} %get-tuple-element.12.codes_in), custom_call_target="tpu_custom_call" | custom-call | tf_op jit(solution)/shard_map/pallas_call | solution.py:427
Async XLA Ops:
  1.7 8.0 %collective-permute-start.14 = (f32[264,128]{1,0:T(8,128)}, f32[264,128]{1,0:T(8,128)S(1)}, u32[]{:S(2)}, u32[]{:S(2)}) collective-permute-start(f32[264,128]{1,0:T(8,128)} %shard_map.46), channel_id=1, source_target_pairs={{0,0},{1,1},{2,2},{3,3},{4,4},{5,5},{6,6},{7,7},{8,8},{9,9},{10,10... | collective-permute-start | bytes 405512 | tf_op jit(solution)/shard_map/ppermute | solution.py:370
  2.7 7.1 %collective-permute-start.10 = (f32[264,128]{1,0:T(8,128)}, f32[264,128]{1,0:T(8,128)S(1)}, u32[]{:S(2)}, u32[]{:S(2)}) collective-permute-start(f32[264,128]{1,0:T(8,128)} %shard_map.46), channel_id=1, source_target_pairs={{0,4},{4,0},{8,12},{12,8},{1,5},{5,1},{9,13},{13,9},{2,6},{6,2},{1... | collective-permute-start | bytes 405512 | tf_op jit(solution)/shard_map/ppermute | solution.py:370
  5.7 7.1 %collective-permute-start.8 = (f32[264,128]{1,0:T(8,128)}, f32[264,128]{1,0:T(8,128)S(1)}, u32[]{:S(2)}, u32[]{:S(2)}) collective-permute-start(f32[264,128]{1,0:T(8,128)} %shard_map.46), channel_id=1, source_target_pairs={{0,2},{2,0},{1,3},{3,1},{4,6},{6,4},{5,7},{7,5},{8,10},{10,8},{9,1... | collective-permute-start | bytes 405512 | tf_op jit(solution)/shard_map/ppermute | solution.py:370
  7.2 8.8 %collective-permute-start = (f32[264,128]{1,0:T(8,128)}, f32[264,128]{1,0:T(8,128)S(1)}, u32[]{:S(2)}, u32[]{:S(2)}) collective-permute-start(f32[264,128]{1,0:T(8,128)} %shard_map.46), channel_id=1, source_target_pairs={{0,8},{4,12},{8,0},{12,4},{1,9},{5,13},{9,1},{13,5},{2,10},{6,14},... | collective-permute-start | bytes 405512 | tf_op jit(solution)/shard_map/ppermute | solution.py:370
  9.8 6.2 %collective-permute-start.15 = (f32[264,128]{1,0:T(8,128)S(1)}, f32[264,128]{1,0:T(8,128)S(1)}, u32[]{:S(2)}, u32[]{:S(2)}) collective-permute-start(f32[264,128]{1,0:T(8,128)S(1)} %collective-permute-done.14.args_15_), channel_id=1, source_target_pairs={{0,1},{1,0},{2,3},{3,2},{4,5},{5,4},{6,7},{7,6},{8,9},{9,8},{10,11... | collective-permute-start | bytes 405512 | tf_op jit(solution)/shard_map/ppermute | solution.py:370
  9.8 7.0 %collective-permute-start.13 = (f32[264,128]{1,0:T(8,128)S(1)}, f32[264,128]{1,0:T(8,128)S(1)}, u32[]{:S(2)}, u32[]{:S(2)}) collective-permute-start(f32[264,128]{1,0:T(8,128)S(1)} %collective-permute-done.10.args_13_), channel_id=1, source_target_pairs={{0,1},{1,0},{2,3},{3,2},{4,5},{5,4},{6,7},{7,6},{8,9},{9,8},{10,11... | collective-permute-start | bytes 405512 | tf_op jit(solution)/shard_map/ppermute | solution.py:370
  10.3 9.2 %collective-permute-start.11 = (f32[264,128]{1,0:T(8,128)S(1)}, f32[264,128]{1,0:T(8,128)S(1)}, u32[]{:S(2)}, u32[]{:S(2)}) collective-permute-start(f32[264,128]{1,0:T(8,128)S(1)} %collective-permute-done.10.args_13_), channel_id=1, source_target_pairs={{0,2},{2,0},{1,3},{3,1},{4,6},{6,4},{5,7},{7,5},{8,10},{10,8},{9,1... | collective-permute-start | bytes 405512 | tf_op jit(solution)/shard_map/ppermute | solution.py:370
  12.8 6.7 %collective-permute-start.9 = (f32[264,128]{1,0:T(8,128)S(1)}, f32[264,128]{1,0:T(8,128)S(1)}, u32[]{:S(2)}, u32[]{:S(2)}) collective-permute-start(f32[264,128]{1,0:T(8,128)S(1)} %collective-permute-done.8.args_9_), channel_id=1, source_target_pairs={{0,1},{1,0},{2,3},{3,2},{4,5},{5,4},{6,7},{7,6},{8,9},{9,8},{10,11... | collective-permute-start | bytes 405512 | tf_op jit(solution)/shard_map/ppermute | solution.py:370
  16.0 6.0 %collective-permute-start.5 = (f32[264,128]{1,0:T(8,128)S(1)}, f32[264,128]{1,0:T(8,128)S(1)}, u32[]{:S(2)}, u32[]{:S(2)}) collective-permute-start(f32[264,128]{1,0:T(8,128)S(1)} %collective-permute-done.args_7_), channel_id=1, source_target_pairs={{0,4},{4,0},{8,12},{12,8},{1,5},{5,1},{9,13},{13,9},{2,6},{6,2},{1... | collective-permute-start | bytes 405512 | tf_op jit(solution)/shard_map/ppermute | solution.py:370
  16.0 7.4 %collective-permute-start.3 = (f32[264,128]{1,0:T(8,128)S(1)}, f32[264,128]{1,0:T(8,128)S(1)}, u32[]{:S(2)}, u32[]{:S(2)}) collective-permute-start(f32[264,128]{1,0:T(8,128)S(1)} %collective-permute-done.args_7_), channel_id=1, source_target_pairs={{0,2},{2,0},{1,3},{3,1},{4,6},{6,4},{5,7},{7,5},{8,10},{10,8},{9,1... | collective-permute-start | bytes 405512 | tf_op jit(solution)/shard_map/ppermute | solution.py:370
  16.7 6.7 %collective-permute-start.1 = (f32[264,128]{1,0:T(8,128)S(1)}, f32[264,128]{1,0:T(8,128)S(1)}, u32[]{:S(2)}, u32[]{:S(2)}) collective-permute-start(f32[264,128]{1,0:T(8,128)S(1)} %collective-permute-done.args_7_), channel_id=1, source_target_pairs={{0,6},{2,4},{4,2},{6,0},{8,14},{10,12},{12,10},{14,8},{1,7},{3,5},... | collective-permute-start | bytes 405512 | tf_op jit(solution)/shard_map/ppermute | solution.py:370
  19.5 4.4 %collective-permute-start.7 = (f32[264,128]{1,0:T(8,128)S(1)}, f32[264,128]{1,0:T(8,128)S(1)}, u32[]{:S(2)}, u32[]{:S(2)}) collective-permute-start(f32[264,128]{1,0:T(8,128)S(1)} %collective-permute-done.args_7_), channel_id=1, source_target_pairs={{0,1},{1,0},{2,3},{3,2},{4,5},{5,4},{6,7},{7,6},{8,9},{9,8},{10,11... | collective-permute-start | bytes 405512 | tf_op jit(solution)/shard_map/ppermute | solution.py:370
  19.5 4.4 %collective-permute-start.12 = (f32[264,128]{1,0:T(8,128)S(1)}, f32[264,128]{1,0:T(8,128)S(1)}, u32[]{:S(2)}, u32[]{:S(2)}) collective-permute-start(f32[264,128]{1,0:T(8,128)S(1)} %collective-permute-done.11.args_11_), channel_id=1, source_target_pairs={{0,1},{1,0},{2,3},{3,2},{4,5},{5,4},{6,7},{7,6},{8,9},{9,8},{10,11... | collective-permute-start | bytes 405512 | tf_op jit(solution)/shard_map/ppermute | solution.py:370
  21.9 2.0 %collective-permute-start.6 = (f32[264,128]{1,0:T(8,128)S(1)}, f32[264,128]{1,0:T(8,128)S(1)}, u32[]{:S(2)}, u32[]{:S(2)}) collective-permute-start(f32[264,128]{1,0:T(8,128)S(1)} %collective-permute-done.5.args_5_), channel_id=1, source_target_pairs={{0,1},{1,0},{2,3},{3,2},{4,5},{5,4},{6,7},{7,6},{8,9},{9,8},{10,11... | collective-permute-start | bytes 405512 | tf_op jit(solution)/shard_map/ppermute | solution.py:370
  23.4 1.4 %collective-permute-start.4 = (f32[264,128]{1,0:T(8,128)S(1)}, f32[264,128]{1,0:T(8,128)S(1)}, u32[]{:S(2)}, u32[]{:S(2)}) collective-permute-start(f32[264,128]{1,0:T(8,128)S(1)} %collective-permute-done.3.args_3_), channel_id=1, source_target_pairs={{0,1},{1,0},{2,3},{3,2},{4,5},{5,4},{6,7},{7,6},{8,9},{9,8},{10,11... | collective-permute-start | bytes 405512 | tf_op jit(solution)/shard_map/ppermute | solution.py:370
  23.4 1.5 %collective-permute-start.2 = (f32[264,128]{1,0:T(8,128)S(1)}, f32[264,128]{1,0:T(8,128)S(1)}, u32[]{:S(2)}, u32[]{:S(2)}) collective-permute-start(f32[264,128]{1,0:T(8,128)S(1)} %collective-permute-done.1.args_1_), channel_id=1, source_target_pairs={{0,1},{1,0},{2,3},{3,2},{4,5},{5,4},{6,7},{7,6},{8,9},{9,8},{10,11... | collective-permute-start | bytes 405512 | tf_op jit(solution)/shard_map/ppermute | solution.py:370
  36.6 2.7 %collective-permute-start.16 = (f32[64,32,128]{2,1,0:T(8,128)S(1)}, f32[64,32,128]{2,1,0:T(8,128)S(1)}, u32[]{:S(2)}, u32[]{:S(2)}) collective-permute-start(f32[64,32,128]{2,1,0:T(8,128)S(1)} %get-tuple-element.10.own), channel_id=1, source_target_pairs={{0,1},{1,0},{2,3},{3,2},{4,5},{5,4},{6,7},{7,6},{8,9},{9,8},{10,11... | collective-permute-start | bytes 3145736 | tf_op jit(solution)/shard_map/ppermute | solution.py:370
  49.5 2.7 %collective-permute-start.17 = (f32[64,32,128]{2,1,0:T(8,128)S(1)}, f32[64,32,128]{2,1,0:T(8,128)S(1)}, u32[]{:S(2)}, u32[]{:S(2)}) collective-permute-start(f32[64,32,128]{2,1,0:T(8,128)S(1)} %shard_map.48.own), channel_id=1, source_target_pairs={{0,1},{1,0},{2,3},{3,2},{4,5},{5,4},{6,7},{7,6},{8,9},{9,8},{10,11... | collective-permute-start | bytes 3145736 | tf_op jit(solution)/shard_map/ppermute | solution.py:370
  56.3 1.6 %collective-permute-start.18 = (f32[16,32,128]{2,1,0:T(8,128)S(1)}, f32[16,32,128]{2,1,0:T(8,128)S(1)}, u32[]{:S(2)}, u32[]{:S(2)}) collective-permute-start(f32[16,32,128]{2,1,0:T(8,128)S(1)} %get-tuple-element.13.own), channel_id=1, source_target_pairs={{0,1},{1,0},{2,3},{3,2},{4,5},{5,4},{6,7},{7,6},{8,9},{9,8},{10,11... | collective-permute-start | bytes 786440 | tf_op jit(solution)/shard_map/ppermute | solution.py:370

commit v2 on v1

--- a/solution.py
+++ b/solution.py
@@ -171,8 +171,7 @@
         self.panel = self.cols * self.tile
         self.tiles = self.rows * self.cols
         self.blocks = self.tiles * self.tile
-        self.half = self.tiles * slots
-        self.strip = self.cols * slots
+        self.half = self.blocks // 2
 
 
 def pack_kernel(sizes, density, left_index, right_index, pair_count, out, blocks, lefts, rights, counts, sems):
@@ -197,10 +196,10 @@
                 live = jnp.where(slot == s, counts[n, q, s], live)
             right = rights[n, q]
             inside = lax.rem(right, sizes.tile)
-            left = lefts[n, q] + (row * sizes.panel if n == 0 else 0)
+            left = lefts[n, q] + (lax.rem(row, sizes.rows // 2) * sizes.panel if n == 0 else 0)
             right = (right - inside) * sizes.cols + col * sizes.tile + inside
             dead = position >= live
-            left = jnp.where(dead, sizes.blocks if n == 0 else sizes.panel, left)
+            left = jnp.where(dead, sizes.half if n == 0 else sizes.panel, left)
             right = jnp.where(dead, sizes.blocks, right)
             codes.append(((live * CODE + left) * CODE + right).astype(F32))
     out[sizes.slots * 32 : sizes.slots * 33] = jnp.concatenate(codes, axis=1)
@@ -209,123 +208,101 @@
         out[s * 32 : s * 32 + 32] = jnp.concatenate([blocks[s, :32], blocks[s, 32:]], axis=1)
 
 
-def first_square_kernel(sizes, offsets, *refs):
+def first_step_kernel(sizes, offsets, *refs):
     pieces, refs = refs[: len(offsets)], refs[len(offsets) :]
-    out, right_ref, codes_out, left_ref, codes, sem, payload, payload_sem = refs
+    out, codes_out, left_ref, right_ref, square_ref, squares, codes, sems = refs
     row, col, rep = lax.axis_index("row"), lax.axis_index("col"), lax.axis_index("rep")
-    fetch = pltpu.make_async_copy(pieces[-1], payload, payload_sem)
-    fetch.start()
-    pieces = pieces[:-1] + (payload,)
-
-    def unpack(piece, offset):
+
+    def place_of(offset):
         m, n, e = offset
         tile = (row ^ m) * sizes.cols + (col ^ n)
-        base = pl.multiple_of(tile * sizes.tile + (rep ^ e) * sizes.slots, sizes.slots)
+        return pl.multiple_of(tile * sizes.tile + (rep ^ e) * sizes.slots, sizes.slots)
+
+    for piece, offset in zip(pieces, offsets):
+        code = piece[sizes.slots * 32 : sizes.slots * 33].astype(jnp.int32)
+        codes_out[pl.ds(place_of(offset), sizes.slots)] = code
+    first = pl.multiple_of(rep * sizes.half, sizes.half)
+    mine = lambda t: t // sizes.half == rep
+    for product, wanted in enumerate((mine, mine, lambda t: t // sizes.panel == row)):
+        order = order_by_count(codes_out[: sizes.blocks], product * sizes.pairs, wanted, sizes.blocks)
+        codes_out[sizes.blocks + product : sizes.blocks + product + 1] = order
+    copies = [
+        pltpu.make_async_copy(codes_out.at[pl.ds(first, sizes.half)], codes.at[pl.ds(0, sizes.half)], sems.at[0]),
+        pltpu.make_async_copy(codes_out.at[pl.ds(sizes.blocks, 8)], codes.at[pl.ds(sizes.half, 8)], sems.at[1]),
+    ]
+    for copy in copies:
+        copy.start()
+
+    zero_block(left_ref, sizes.half, right_ref, sizes.blocks)
+    zero_block(square_ref, sizes.half, None, None)
+    for piece, offset in zip(pieces, offsets):
+        base = place_of(offset)
         for s in range(sizes.slots):
-            twice = spread(piece[s * 32 : s * 32 + 32])
-            store_left(left_ref, base + s, twice)
-            store_right(right_ref, base + s, twice)
-
-    def unpack_codes(piece, offset):
-        m, n, e = offset
-        if e == 0:
-            place = pl.multiple_of(((row ^ m) * sizes.cols + (col ^ n)) * sizes.slots, sizes.slots)
-            codes_out[pl.ds(place, sizes.slots)] = piece[sizes.slots * 32 : sizes.slots * 33].astype(jnp.int32)
-
-    fetch.wait()
-    for piece, offset in zip(pieces, offsets):
-        unpack_codes(piece, offset)
-    mine = lambda place: place < sizes.half
-    wanted = (mine, mine, lambda place: mine(place) & (place // sizes.strip == row))
-    for product, choice in enumerate(wanted):
-        order = order_by_count(codes_out[: sizes.blocks], product * sizes.pairs, choice, sizes.blocks)
-        codes_out[sizes.half + product : sizes.half + product + 1] = order
-    copy = pltpu.make_async_copy(codes_out.at[pl.ds(0, sizes.half + 8)], codes, sem)
-    copy.start()
-    zero_block(left_ref, sizes.blocks, right_ref, sizes.blocks)
-    for piece, offset in zip(pieces, offsets):
-        unpack(piece, offset)
-    copy.wait()
-
-    def finish(place, twice):
-        out[place] = pack(twice)
-
-    ordered_products(sizes, codes, sizes.half, 0, 0, sizes.half, 16, left_ref, right_ref, finish)
-
-
-def first_cube_kernel(sizes, own, other, right_ref, codes_in, out, left_ref, codes, sem):
-    copy = pltpu.make_async_copy(codes_in.at[pl.ds(0, sizes.half + 8)], codes, sem)
-    copy.start()
-    rep = lax.axis_index("rep")
-    zero_block(left_ref, sizes.blocks, None, None)
-
-    def prepare_tile(i, carry):
-        for e, source in ((rep, own), (1 - rep, other)):
-            for s in range(sizes.slots):
-                store_left(
-                    left_ref, (i * sizes.reps + e) * sizes.slots + s, spread(source[i * sizes.slots + s])
-                )
-        return carry
-
-    lax.fori_loop(0, sizes.tiles, prepare_tile, 0)
-    copy.wait()
-
-    def finish(place, twice):
-        out[place] = 3.0 * own[place] - 2.0 * pack(twice)
-
-    ordered_products(sizes, codes, sizes.half, 0, 1, sizes.half, 16, left_ref, right_ref, finish)
-
-
-def last_square_kernel(sizes, own, other, codes_in, out, right_ref, left_ref, codes, sems):
-    row, rep = lax.axis_index("row"), lax.axis_index("rep")
-    first = pl.multiple_of(row * sizes.strip, sizes.strip)
+            store_right(right_ref, base + s, spread(piece[s * 32 : s * 32 + 32]))
+    for far in range(2):
+
+        @pl.when(row // (sizes.rows // 2) ^ far == rep)
+        def _():
+            for piece, offset in zip(pieces, offsets):
+                if offset[0] // (sizes.rows // 2) == far:
+                    base = place_of(offset) - first
+                    for s in range(sizes.slots):
+                        store_left(left_ref, base + s, spread(piece[s * 32 : s * 32 + 32]))
+
+    for copy in copies:
+        copy.wait()
+
+    def finish_square(place, twice):
+        store_left(square_ref, place, twice)
+        squares[place] = pack(twice)
+
+    def finish_cube(place, twice):
+        out[place] = 3.0 * squares[place] - 2.0 * pack(twice)
+
+    ordered_products(sizes, codes, sizes.half, first, 0, sizes.half, 16, left_ref, right_ref, finish_square)
+    ordered_products(sizes, codes, sizes.half, first, 1, sizes.half, 16, square_ref, right_ref, finish_cube)
+
+
+def last_step_kernel(sizes, own, other, codes_in, out, left_ref, right_ref, square_ref, squares, codes, sems):
+    row, col, rep = lax.axis_index("row"), lax.axis_index("col"), lax.axis_index("rep")
+    first = pl.multiple_of(row * sizes.panel, sizes.panel)
     copies = [
-        pltpu.make_async_copy(codes_in.at[pl.ds(first, sizes.strip)], codes.at[pl.ds(0, sizes.strip)], sems.at[0]),
-        pltpu.make_async_copy(codes_in.at[pl.ds(sizes.half, 8)], codes.at[pl.ds(sizes.strip, 8)], sems.at[1]),
+        pltpu.make_async_copy(codes_in.at[pl.ds(first, sizes.panel)], codes.at[pl.ds(0, sizes.panel)], sems.at[0]),
+        pltpu.make_async_copy(codes_in.at[pl.ds(sizes.blocks, 8)], codes.at[pl.ds(sizes.panel, 8)], sems.at[1]),
     ]
     for copy in copies:
         copy.start()
     zero_block(left_ref, sizes.panel, right_ref, sizes.blocks)
-
-    def prepare_tile(i, carry):
-        for e, source in ((rep, own), (1 - rep, other)):
-            for s in range(sizes.slots):
-                store_right(
-                    right_ref, (i * sizes.reps + e) * sizes.slots + s, spread(source[i * sizes.slots + s])
-                )
-        return carry
-
-    lax.fori_loop(0, sizes.tiles, prepare_tile, 0)
-    for n in range(sizes.cols):
-        for e, source in ((rep, own), (1 - rep, other)):
-            for s in range(sizes.slots):
-                twice = spread(source[(row * sizes.cols + n) * sizes.slots + s])
-                store_left(left_ref, (n * sizes.reps + e) * sizes.slots + s, twice)
+    zero_block(square_ref, sizes.panel, None, None)
+    unroll = 2 * sizes.slots
+    for part, source in ((rep, own), (1 - rep, other)):
+
+        def prepare_right(i, carry):
+            for s in range(unroll):
+                at = i * unroll + s
+                store_right(right_ref, part * sizes.half + at, spread(source[at]))
+            return carry
+
+        lax.fori_loop(0, sizes.half // unroll, prepare_right, 0)
+
+        @pl.when(row // (sizes.rows // 2) == part)
+        def _():
+            base = lax.rem(row, sizes.rows // 2) * sizes.panel
+            for s in range(sizes.panel):
+                store_left(left_ref, s, spread(source[base + s]))
+
     for copy in copies:
         copy.wait()
 
-    def finish(place, twice):
-        out[place] = pack(twice)
-
-    ordered_products(sizes, codes, sizes.strip, first, 2, sizes.strip, 8, left_ref, right_ref, finish)
-
-
-def last_cube_kernel(sizes, own, other, right_ref, codes_in, out, left_ref, codes, sem):
-    row, col, rep = lax.axis_index("row"), lax.axis_index("col"), lax.axis_index("rep")
-    base = pl.multiple_of((row * sizes.cols + col) * sizes.slots, sizes.slots)
-    copy = pltpu.make_async_copy(codes_in.at[pl.ds(base, sizes.slots)], codes, sem)
-    copy.start()
-    zero_block(left_ref, sizes.panel, None, None)
-    for n in range(sizes.cols):
-        for e, source in ((rep, own), (1 - rep, other)):
-            for s in range(sizes.slots):
-                twice = spread(source[n * sizes.slots + s])
-                store_left(left_ref, (n * sizes.reps + e) * sizes.slots + s, twice)
-    copy.wait()
+    def finish_square(place, twice):
+        store_left(square_ref, place, twice)
+        squares[place] = pack(twice)
+
+    ordered_products(sizes, codes, sizes.panel, first, 2, sizes.panel, 16, left_ref, right_ref, finish_square)
+    base = (col * sizes.reps + rep) * sizes.slots
     for s in range(sizes.slots):
-        cube = fold(block_products(codes, s, 3 * sizes.pairs, sizes.pairs, left_ref, right_ref))
-        square = spread(own[col * sizes.slots + s])
-        out[s] = (3.0 * square - 2.0 * cube)[:, :64]
+        cube = fold(block_products(codes, base + s, 3 * sizes.pairs, sizes.pairs, square_ref, right_ref))
+        out[s] = (3.0 * spread(squares[base + s]) - 2.0 * cube)[:, :64]
 
 
 def call(kernel, sizes, outs, in_specs, out_specs, scratch, limit=40):
@@ -343,12 +320,17 @@
     width = density.shape[1]
     index_shape = (STEPS, 2, sizes.slots, sizes.pairs)
     code_shape = (sizes.blocks + 8, STEPS * 2 * sizes.pairs)
-    packed = lambda count: jax.ShapeDtypeStruct((count, 32, 128), F32)
-    rights = jax.ShapeDtypeStruct((sizes.blocks + 1, 64, 128), BF16)
-    code_scratch = [
-        pltpu.SMEM((sizes.half + 8, code_shape[1]), jnp.int32),
-        pltpu.SemaphoreType.DMA,
-    ]
+    packed = jax.ShapeDtypeStruct((sizes.half, 32, 128), F32)
+
+    def scratch(blocks):
+        return [
+            pltpu.VMEM((blocks + 1, 128, 128), BF16),
+            pltpu.VMEM((sizes.blocks + 1, 64, 128), BF16),
+            pltpu.VMEM((blocks + 1, 128, 128), BF16),
+            pltpu.VMEM((blocks, 32, 128), F32),
+            pltpu.SMEM((blocks + 8, code_shape[1]), jnp.int32),
+            pltpu.SemaphoreType.DMA((2,)),
+        ]
 
     payload = call(
         pack_kernel,
@@ -393,49 +375,22 @@
     ]
     pieces = [pair for (m, n, e), piece in own for pair in (((m, n, e), piece), ((m, n, 1), rep_swap(piece)))]
     offsets, pieces = zip(*pieces[::-1])
-
-    square, right, codes = call(
-        lambda *args: first_square_kernel(args[0], offsets, *args[1:]),
+    current, codes = call(
+        lambda *args: first_step_kernel(args[0], offsets, *args[1:]),
         sizes,
-        [packed(sizes.half), rights, jax.ShapeDtypeStruct(code_shape, jnp.int32)],
-        [VMEM] * (len(pieces) - 1) + [ANY],
-        [VMEM] * 3,
-        [pltpu.VMEM((sizes.blocks + 1, 128, 128), BF16)]
-        + code_scratch
-        + [pltpu.VMEM(payload.shape, F32), pltpu.SemaphoreType.DMA],
+        [packed, jax.ShapeDtypeStruct(code_shape, jnp.int32)],
+        [VMEM] * len(pieces),
+        [VMEM] * 2,
+        scratch(sizes.half),
     )(*pieces)
-    current = call(
-        first_cube_kernel,
-        sizes,
-        packed(sizes.half),
-        [VMEM] * 3 + [ANY],
-        VMEM,
-        [pltpu.VMEM((sizes.blocks + 1, 128, 128), BF16)] + code_scratch,
-    )(square, rep_swap(square), right, codes)
-    square, right = call(
-        last_square_kernel,
-        sizes,
-        [packed(sizes.cols * sizes.slots), rights],
-        [VMEM] * 2 + [ANY],
-        [VMEM] * 2,
-        [
-            pltpu.VMEM((sizes.panel + 1, 128, 128), BF16),
-            pltpu.SMEM((sizes.strip + 8, code_shape[1]), jnp.int32),
-            pltpu.SemaphoreType.DMA((2,)),
-        ],
-    )(current, rep_swap(current), codes)
     return call(
-        last_cube_kernel,
+        last_step_kernel,
         sizes,
         jax.ShapeDtypeStruct(density.shape, F32),
-        [VMEM] * 3 + [ANY],
+        [VMEM] * 2 + [ANY],
         VMEM,
-        [
-            pltpu.VMEM((sizes.panel + 1, 128, 128), BF16),
-            pltpu.SMEM((sizes.slots, code_shape[1]), jnp.int32),
-            pltpu.SemaphoreType.DMA,
-        ],
-    )(square, rep_swap(square), right, codes)
+        scratch(sizes.panel),
+    )(current, rep_swap(current), codes)
 
 
 def solution(mesh):

time: 61.8 us -> 58.4 us (0.945); the launches traced: 60.9 us -> 58.5 us
  waiting for transfers between devices: 13.3 us -> 9.71 us
  Pallas kernels: 30.5 us -> 31.8 us
    ppermute x19 -> x17, waiting for transfers between devices: 13.3 us -> 9.71 us  [swap(): return lax.ppermute(value, axes, [(i, i ^ mask) for i in range(size)])]
    pallas_call x4 -> x2, Pallas kernels: 28.8 us -> 30.1 us  [the longest x1 20.9 us: whole_form(): call(lambda *args: first_step_kernel(args[0], offsets, *args[1:]), sizes,...]
    ppermute x19 -> x17, starting transfers between devices: 16.9 us -> 16.7 us  [swap(): return lax.ppermute(value, axes, [(i, i ^ mask) for i in range(size)])]
  transfers between devices with their start and end apart: 19 -> 17, of which waited for: 8 -> 6; matrix products, arithmetic and copies ran while one was open for 0% -> 0% of each run, Pallas kernels for 0% -> 0%
where the time goes in v2:
time: 58.4 us; the launch traced here: 58.5 us
  Pallas kernels  31.8 us (54%)
  starting transfers between devices  16.7 us (29%)
  waiting for transfers between devices  9.71 us (17%)
    pallas_call x1, Pallas kernels, whole_form(): call(lambda *args: first_step_kernel(args[0], offsets, *args[1:]), sizes,...  20.9 us
    ppermute x17, starting transfers between devices, swap(): return lax.ppermute(value, axes, [(i, i ^ mask) for i in range(size)])  16.7 us
    ppermute x17, waiting for transfers between devices, swap(): return lax.ppermute(value, axes, [(i, i ^ mask) for i in range(size)])  9.71 us
    pallas_call x1, Pallas kernels, whole_form(): call(last_step_kernel, sizes, jax.ShapeDtypeStruct(density.shape, F32), [...  9.17 us
    pallas_call x1, Pallas kernels, whole_form(): call(pack_kernel, sizes, jax.ShapeDtypeStruct((sizes.slots * 33, 128), F3...  1.74 us
  transfers between devices with their start and end apart: 17, of which 6 were waited for; matrix products, arithmetic and copies ran while one was open for 0% of the time, Pallas kernels for 0%

profile of v2, /device:TPU:0, one launch (start us, length us, event | category | flops | bytes accessed | tf_op | source)
XLA Modules:
  0.0 58.5 jit_solution(5993937436093859514)
XLA Ops:
  0.0 1.7 %shard_map.46 = f32[264,128]{1,0:T(8,128)} custom-call(f32[8,64,64]{2,1,0:T(8,128)} %density.1, s32[2,2,8,32]{3,2,1,0:T(8,128)} %left_index.1, s32[2,2,8,32]{3,2,1,0:T(8,128)} %right_index.1, s32[2,2,8]{2,1,0:T(2,128)} %pair_count.1), custom_call_target="tpu_custom_call" | custom-call | tf_op jit(solution)/shard_map/pallas_call | solution.py:335
  1.7 0.9 %collective-permute-start.14 = (f32[264,128]{1,0:T(8,128)}, f32[264,128]{1,0:T(8,128)S(1)}, u32[]{:S(2)}, u32[]{:S(2)}) collective-permute-start(f32[264,128]{1,0:T(8,128)} %shard_map.46), channel_id=1, source_target_pairs={{0,0},{1,1},{2,2},{3,3},{4,4},{5,5},{6,6},{7,7},{8,8},{9,9},{10,10... | collective-permute-start | bytes 405512 | tf_op jit(solution)/shard_map/ppermute | solution.py:352
  2.7 3.0 %collective-permute-start.10 = (f32[264,128]{1,0:T(8,128)}, f32[264,128]{1,0:T(8,128)S(1)}, u32[]{:S(2)}, u32[]{:S(2)}) collective-permute-start(f32[264,128]{1,0:T(8,128)} %shard_map.46), channel_id=1, source_target_pairs={{0,4},{4,0},{8,12},{12,8},{1,5},{5,1},{9,13},{13,9},{2,6},{6,2},{1... | collective-permute-start | bytes 405512 | tf_op jit(solution)/shard_map/ppermute | solution.py:352
  5.7 1.5 %collective-permute-start.8 = (f32[264,128]{1,0:T(8,128)}, f32[264,128]{1,0:T(8,128)S(1)}, u32[]{:S(2)}, u32[]{:S(2)}) collective-permute-start(f32[264,128]{1,0:T(8,128)} %shard_map.46), channel_id=1, source_target_pairs={{0,2},{2,0},{1,3},{3,1},{4,6},{6,4},{5,7},{7,5},{8,10},{10,8},{9,1... | collective-permute-start | bytes 405512 | tf_op jit(solution)/shard_map/ppermute | solution.py:352
  7.2 2.6 %collective-permute-start = (f32[264,128]{1,0:T(8,128)}, f32[264,128]{1,0:T(8,128)S(1)}, u32[]{:S(2)}, u32[]{:S(2)}) collective-permute-start(f32[264,128]{1,0:T(8,128)} %shard_map.46), channel_id=1, source_target_pairs={{0,8},{4,12},{8,0},{12,4},{1,9},{5,13},{9,1},{13,5},{2,10},{6,14},... | collective-permute-start | bytes 405512 | tf_op jit(solution)/shard_map/ppermute | solution.py:352
  9.8 0.0 collective-permute-done.14.args_15_
  9.8 0.0 collective-permute-start.15
  9.8 0.0 collective-permute-done.10.args_13_
  9.8 0.5 collective-permute-start.13
  10.3 2.5 %collective-permute-start.11 = (f32[264,128]{1,0:T(8,128)S(1)}, f32[264,128]{1,0:T(8,128)S(1)}, u32[]{:S(2)}, u32[]{:S(2)}) collective-permute-start(f32[264,128]{1,0:T(8,128)S(1)} %collective-permute-done.10.args_13_), channel_id=1, source_target_pairs={{0,2},{2,0},{1,3},{3,1},{4,6},{6,4},{5,7},{7,5},{8,10},{10,8},{9,1... | collective-permute-start | bytes 405512 | tf_op jit(solution)/shard_map/ppermute | solution.py:352
  12.8 0.0 collective-permute-done.8.args_9_
  12.8 0.2 collective-permute-start.9
  13.0 3.0 %collective-permute-done.args_7_ = f32[264,128]{1,0:T(8,128)S(1)} collective-permute-done((f32[264,128]{1,0:T(8,128)}, f32[264,128]{1,0:T(8,128)S(1)}, u32[]{:S(2)}, u32[]{:S(2)}) %collective-permute-start) | collective-permute-done | bytes 135200 | tf_op jit(solution)/shard_map/ppermute | solution.py:352
  16.0 0.0 collective-permute-start.5
  16.0 0.0 collective-permute-done.15.args_14_
  16.0 0.8 %collective-permute-start.3 = (f32[264,128]{1,0:T(8,128)S(1)}, f32[264,128]{1,0:T(8,128)S(1)}, u32[]{:S(2)}, u32[]{:S(2)}) collective-permute-start(f32[264,128]{1,0:T(8,128)S(1)} %collective-permute-done.args_7_), channel_id=1, source_target_pairs={{0,2},{2,0},{1,3},{3,1},{4,6},{6,4},{5,7},{7,5},{8,10},{10,8},{9,1... | collective-permute-start | bytes 405512 | tf_op jit(solution)/shard_map/ppermute | solution.py:352
  16.7 0.0 collective-permute-done.13.args_12_
  16.7 2.7 %collective-permute-start.1 = (f32[264,128]{1,0:T(8,128)S(1)}, f32[264,128]{1,0:T(8,128)S(1)}, u32[]{:S(2)}, u32[]{:S(2)}) collective-permute-start(f32[264,128]{1,0:T(8,128)S(1)} %collective-permute-done.args_7_), channel_id=1, source_target_pairs={{0,6},{2,4},{4,2},{6,0},{8,14},{10,12},{12,10},{14,8},{1,7},{3,5},... | collective-permute-start | bytes 405512 | tf_op jit(solution)/shard_map/ppermute | solution.py:352
  19.5 0.0 collective-permute-done.11.args_11_
  19.5 0.0 collective-permute-start.7
  19.5 0.0 collective-permute-done.9.args_8_
  19.5 0.5 collective-permute-start.12
  20.0 2.0 %collective-permute-done.5.args_5_ = f32[264,128]{1,0:T(8,128)S(1)} collective-permute-done((f32[264,128]{1,0:T(8,128)S(1)}, f32[264,128]{1,0:T(8,128)S(1)}, u32[]{:S(2)}, u32[]{:S(2)}) %collective-permute-start.5) | collective-permute-done | bytes 135200 | tf_op jit(solution)/shard_map/ppermute | solution.py:352
  21.9 0.0 collective-permute-start.6
  21.9 1.5 %collective-permute-done.3.args_3_ = f32[264,128]{1,0:T(8,128)S(1)} collective-permute-done((f32[264,128]{1,0:T(8,128)S(1)}, f32[264,128]{1,0:T(8,128)S(1)}, u32[]{:S(2)}, u32[]{:S(2)}) %collective-permute-start.3) | collective-permute-done | bytes 135200 | tf_op jit(solution)/shard_map/ppermute | solution.py:352
  23.4 0.0 collective-permute-start.4
  23.4 0.0 collective-permute-done.1.args_1_
  23.4 0.5 collective-permute-start.2
  23.9 0.0 collective-permute-done.7.args_6_
  23.9 0.0 collective-permute-done.12.args_10_
  23.9 0.0 collective-permute-done.6.args_4_
  23.9 0.8 %collective-permute-done.4.args_2_ = f32[264,128]{1,0:T(8,128)S(1)} collective-permute-done((f32[264,128]{1,0:T(8,128)S(1)}, f32[264,128]{1,0:T(8,128)S(1)}, u32[]{:S(2)}, u32[]{:S(2)}) %collective-permute-start.4) | collective-permute-done | bytes 135200 | tf_op jit(solution)/shard_map/ppermute | solution.py:352
  24.7 0.2 collective-permute-done.2.args_0_
  24.9 20.9 %shard_map.47 = (f32[64,32,128]{2,1,0:T(8,128)S(1)}, s32[136,128]{1,0:T(8,128)S(1)}) custom-call(f32[264,128]{1,0:T(8,128)S(1)} %collective-permute-done.2.args_0_, f32[264,128]{1,0:T(8,128)S(1)} %collective-permute-done.1.args_1_, f32[264,128]{1,0:T(8,128)S(1)} %collective-permute-done.4.args_2_, f32[264,128]{1,0:T(8,128)S(1)} %collective-permute-done.3.args_3_, ...), custom_call_target="tpu_custom_call" | custom-call | tf_op jit(solution)/shard_map/pallas_call | solution.py:378
  45.9 1.0 %collective-permute-start.16 = (f32[64,32,128]{2,1,0:T(8,128)S(1)}, f32[64,32,128]{2,1,0:T(8,128)S(1)}, u32[]{:S(2)}, u32[]{:S(2)}) collective-permute-start(f32[64,32,128]{2,1,0:T(8,128)S(1)} %get-tuple-element.7.own), channel_id=1, source_target_pairs={{0,1},{1,0},{2,3},{3,2},{4,5},{5,4},{6,7},{7,6},{8,9},{9,8},{10,11... | collective-permute-start | bytes 3145736 | tf_op jit(solution)/shard_map/ppermute | solution.py:352
  46.9 2.3 %collective-permute-done.16.other = f32[64,32,128]{2,1,0:T(8,128)S(1)} collective-permute-done((f32[64,32,128]{2,1,0:T(8,128)S(1)}, f32[64,32,128]{2,1,0:T(8,128)S(1)}, u32[]{:S(2)}, u32[]{:S(2)}) %collective-permute-start.16) | collective-permute-done | bytes 1048608 | tf_op jit(solution)/shard_map/ppermute | solution.py:352
  49.1 9.2 %shard_map.48 = f32[8,64,64]{2,1,0:T(8,128)} custom-call(f32[64,32,128]{2,1,0:T(8,128)S(1)} %get-tuple-element.7.own, f32[64,32,128]{2,1,0:T(8,128)S(1)} %collective-permute-done.16.other, s32[136,128]{1,0:T(8,128)S(1)} %get-tuple-element.8.codes_in), custom_call_target="tpu_custom_call" | custom-call | tf_op jit(solution)/shard_map/pallas_call | solution.py:386
Async XLA Ops:
  1.7 8.0 %collective-permute-start.14 = (f32[264,128]{1,0:T(8,128)}, f32[264,128]{1,0:T(8,128)S(1)}, u32[]{:S(2)}, u32[]{:S(2)}) collective-permute-start(f32[264,128]{1,0:T(8,128)} %shard_map.46), channel_id=1, source_target_pairs={{0,0},{1,1},{2,2},{3,3},{4,4},{5,5},{6,6},{7,7},{8,8},{9,9},{10,10... | collective-permute-start | bytes 405512 | tf_op jit(solution)/shard_map/ppermute | solution.py:352
  2.7 7.1 %collective-permute-start.10 = (f32[264,128]{1,0:T(8,128)}, f32[264,128]{1,0:T(8,128)S(1)}, u32[]{:S(2)}, u32[]{:S(2)}) collective-permute-start(f32[264,128]{1,0:T(8,128)} %shard_map.46), channel_id=1, source_target_pairs={{0,4},{4,0},{8,12},{12,8},{1,5},{5,1},{9,13},{13,9},{2,6},{6,2},{1... | collective-permute-start | bytes 405512 | tf_op jit(solution)/shard_map/ppermute | solution.py:352
  5.7 7.1 %collective-permute-start.8 = (f32[264,128]{1,0:T(8,128)}, f32[264,128]{1,0:T(8,128)S(1)}, u32[]{:S(2)}, u32[]{:S(2)}) collective-permute-start(f32[264,128]{1,0:T(8,128)} %shard_map.46), channel_id=1, source_target_pairs={{0,2},{2,0},{1,3},{3,1},{4,6},{6,4},{5,7},{7,5},{8,10},{10,8},{9,1... | collective-permute-start | bytes 405512 | tf_op jit(solution)/shard_map/ppermute | solution.py:352
  7.2 8.8 %collective-permute-start = (f32[264,128]{1,0:T(8,128)}, f32[264,128]{1,0:T(8,128)S(1)}, u32[]{:S(2)}, u32[]{:S(2)}) collective-permute-start(f32[264,128]{1,0:T(8,128)} %shard_map.46), channel_id=1, source_target_pairs={{0,8},{4,12},{8,0},{12,4},{1,9},{5,13},{9,1},{13,5},{2,10},{6,14},... | collective-permute-start | bytes 405512 | tf_op jit(solution)/shard_map/ppermute | solution.py:352
  9.8 6.2 %collective-permute-start.15 = (f32[264,128]{1,0:T(8,128)S(1)}, f32[264,128]{1,0:T(8,128)S(1)}, u32[]{:S(2)}, u32[]{:S(2)}) collective-permute-start(f32[264,128]{1,0:T(8,128)S(1)} %collective-permute-done.14.args_15_), channel_id=1, source_target_pairs={{0,1},{1,0},{2,3},{3,2},{4,5},{5,4},{6,7},{7,6},{8,9},{9,8},{10,11... | collective-permute-start | bytes 405512 | tf_op jit(solution)/shard_map/ppermute | solution.py:352
  9.8 7.0 %collective-permute-start.13 = (f32[264,128]{1,0:T(8,128)S(1)}, f32[264,128]{1,0:T(8,128)S(1)}, u32[]{:S(2)}, u32[]{:S(2)}) collective-permute-start(f32[264,128]{1,0:T(8,128)S(1)} %collective-permute-done.10.args_13_), channel_id=1, source_target_pairs={{0,1},{1,0},{2,3},{3,2},{4,5},{5,4},{6,7},{7,6},{8,9},{9,8},{10,11... | collective-permute-start | bytes 405512 | tf_op jit(solution)/shard_map/ppermute | solution.py:352
  10.3 9.2 %collective-permute-start.11 = (f32[264,128]{1,0:T(8,128)S(1)}, f32[264,128]{1,0:T(8,128)S(1)}, u32[]{:S(2)}, u32[]{:S(2)}) collective-permute-start(f32[264,128]{1,0:T(8,128)S(1)} %collective-permute-done.10.args_13_), channel_id=1, source_target_pairs={{0,2},{2,0},{1,3},{3,1},{4,6},{6,4},{5,7},{7,5},{8,10},{10,8},{9,1... | collective-permute-start | bytes 405512 | tf_op jit(solution)/shard_map/ppermute | solution.py:352
  12.8 6.7 %collective-permute-start.9 = (f32[264,128]{1,0:T(8,128)S(1)}, f32[264,128]{1,0:T(8,128)S(1)}, u32[]{:S(2)}, u32[]{:S(2)}) collective-permute-start(f32[264,128]{1,0:T(8,128)S(1)} %collective-permute-done.8.args_9_), channel_id=1, source_target_pairs={{0,1},{1,0},{2,3},{3,2},{4,5},{5,4},{6,7},{7,6},{8,9},{9,8},{10,11... | collective-permute-start | bytes 405512 | tf_op jit(solution)/shard_map/ppermute | solution.py:352
  16.0 6.0 %collective-permute-start.5 = (f32[264,128]{1,0:T(8,128)S(1)}, f32[264,128]{1,0:T(8,128)S(1)}, u32[]{:S(2)}, u32[]{:S(2)}) collective-permute-start(f32[264,128]{1,0:T(8,128)S(1)} %collective-permute-done.args_7_), channel_id=1, source_target_pairs={{0,4},{4,0},{8,12},{12,8},{1,5},{5,1},{9,13},{13,9},{2,6},{6,2},{1... | collective-permute-start | bytes 405512 | tf_op jit(solution)/shard_map/ppermute | solution.py:352
  16.0 7.4 %collective-permute-start.3 = (f32[264,128]{1,0:T(8,128)S(1)}, f32[264,128]{1,0:T(8,128)S(1)}, u32[]{:S(2)}, u32[]{:S(2)}) collective-permute-start(f32[264,128]{1,0:T(8,128)S(1)} %collective-permute-done.args_7_), channel_id=1, source_target_pairs={{0,2},{2,0},{1,3},{3,1},{4,6},{6,4},{5,7},{7,5},{8,10},{10,8},{9,1... | collective-permute-start | bytes 405512 | tf_op jit(solution)/shard_map/ppermute | solution.py:352
  16.7 6.7 %collective-permute-start.1 = (f32[264,128]{1,0:T(8,128)S(1)}, f32[264,128]{1,0:T(8,128)S(1)}, u32[]{:S(2)}, u32[]{:S(2)}) collective-permute-start(f32[264,128]{1,0:T(8,128)S(1)} %collective-permute-done.args_7_), channel_id=1, source_target_pairs={{0,6},{2,4},{4,2},{6,0},{8,14},{10,12},{12,10},{14,8},{1,7},{3,5},... | collective-permute-start | bytes 405512 | tf_op jit(solution)/shard_map/ppermute | solution.py:352
  19.5 4.4 %collective-permute-start.7 = (f32[264,128]{1,0:T(8,128)S(1)}, f32[264,128]{1,0:T(8,128)S(1)}, u32[]{:S(2)}, u32[]{:S(2)}) collective-permute-start(f32[264,128]{1,0:T(8,128)S(1)} %collective-permute-done.args_7_), channel_id=1, source_target_pairs={{0,1},{1,0},{2,3},{3,2},{4,5},{5,4},{6,7},{7,6},{8,9},{9,8},{10,11... | collective-permute-start | bytes 405512 | tf_op jit(solution)/shard_map/ppermute | solution.py:352
  19.5 4.4 %collective-permute-start.12 = (f32[264,128]{1,0:T(8,128)S(1)}, f32[264,128]{1,0:T(8,128)S(1)}, u32[]{:S(2)}, u32[]{:S(2)}) collective-permute-start(f32[264,128]{1,0:T(8,128)S(1)} %collective-permute-done.11.args_11_), channel_id=1, source_target_pairs={{0,1},{1,0},{2,3},{3,2},{4,5},{5,4},{6,7},{7,6},{8,9},{9,8},{10,11... | collective-permute-start | bytes 405512 | tf_op jit(solution)/shard_map/ppermute | solution.py:352
  21.9 2.0 %collective-permute-start.6 = (f32[264,128]{1,0:T(8,128)S(1)}, f32[264,128]{1,0:T(8,128)S(1)}, u32[]{:S(2)}, u32[]{:S(2)}) collective-permute-start(f32[264,128]{1,0:T(8,128)S(1)} %collective-permute-done.5.args_5_), channel_id=1, source_target_pairs={{0,1},{1,0},{2,3},{3,2},{4,5},{5,4},{6,7},{7,6},{8,9},{9,8},{10,11... | collective-permute-start | bytes 405512 | tf_op jit(solution)/shard_map/ppermute | solution.py:352
  23.4 1.4 %collective-permute-start.4 = (f32[264,128]{1,0:T(8,128)S(1)}, f32[264,128]{1,0:T(8,128)S(1)}, u32[]{:S(2)}, u32[]{:S(2)}) collective-permute-start(f32[264,128]{1,0:T(8,128)S(1)} %collective-permute-done.3.args_3_), channel_id=1, source_target_pairs={{0,1},{1,0},{2,3},{3,2},{4,5},{5,4},{6,7},{7,6},{8,9},{9,8},{10,11... | collective-permute-start | bytes 405512 | tf_op jit(solution)/shard_map/ppermute | solution.py:352
  23.4 1.5 %collective-permute-start.2 = (f32[264,128]{1,0:T(8,128)S(1)}, f32[264,128]{1,0:T(8,128)S(1)}, u32[]{:S(2)}, u32[]{:S(2)}) collective-permute-start(f32[264,128]{1,0:T(8,128)S(1)} %collective-permute-done.1.args_1_), channel_id=1, source_target_pairs={{0,1},{1,0},{2,3},{3,2},{4,5},{5,4},{6,7},{7,6},{8,9},{9,8},{10,11... | collective-permute-start | bytes 405512 | tf_op jit(solution)/shard_map/ppermute | solution.py:352
  45.9 3.3 %collective-permute-start.16 = (f32[64,32,128]{2,1,0:T(8,128)S(1)}, f32[64,32,128]{2,1,0:T(8,128)S(1)}, u32[]{:S(2)}, u32[]{:S(2)}) collective-permute-start(f32[64,32,128]{2,1,0:T(8,128)S(1)} %get-tuple-element.7.own), channel_id=1, source_target_pairs={{0,1},{1,0},{2,3},{3,2},{4,5},{5,4},{6,7},{7,6},{8,9},{9,8},{10,11... | collective-permute-start | bytes 3145736 | tf_op jit(solution)/shard_map/ppermute | solution.py:352

commit v3 on v2

--- a/solution.py
+++ b/solution.py
@@ -94,18 +94,6 @@
     ref[at] = jnp.where(left_lanes(64), high.astype(F32), low).astype(BF16)
 
 
-def prepare(source, first, count, base, left_ref, right_ref, unroll=8):
-    def body(i, carry):
-        twice = spread(source[first + i])
-        if left_ref is not None:
-            store_left(left_ref, base + i, twice)
-        if right_ref is not None:
-            store_right(right_ref, base + i, twice)
-        return carry
-
-    lax.fori_loop(0, count, body, 0, unroll=unroll)
-
-
 def zero_block(left_ref, left_at, right_ref, right_at):
     if left_ref is not None:
         left_ref[left_at] = jnp.zeros((128, 128), BF16)
@@ -113,29 +101,29 @@
         right_ref[right_at] = jnp.zeros((64, 128), BF16)
 
 
-def block_products(codes, at, lane, pairs, left_ref, right_ref):
+def block_products(codes, places, lane, pairs, left_ref, right_ref):
     mask = left_lanes(128)
-    total = jnp.zeros((128, 128), F32)
+    totals = [jnp.zeros((128, 128), F32) for _ in places]
     for start in range(0, pairs, CHUNK):
-        lefts, rights = [], []
-        for p in range(start, start + CHUNK):
-            code = codes[at, lane + p]
-            lefts.append(left_ref[(code >> 8) & (CODE - 1)])
-            rights.append(right_ref[code & (CODE - 1)])
-        left = jnp.concatenate(
-            [jnp.where(mask, lefts[0], lefts[1]), jnp.where(mask, lefts[2], lefts[3])], axis=1
-        )
-        right = jnp.concatenate(rights, axis=0)
-        total = total + jnp.dot(left, right, preferred_element_type=F32)
-    return total
-
-
-def fold(total):
-    both = total[:64] + total[64:]
+        for i, place in enumerate(places):
+            lefts, rights = [], []
+            for p in range(start, start + CHUNK):
+                code = codes[place, lane + p]
+                lefts.append(left_ref[(code >> 8) & (CODE - 1)])
+                rights.append(right_ref[code & (CODE - 1)])
+            left = jnp.concatenate(
+                [jnp.where(mask, lefts[0], lefts[1]), jnp.where(mask, lefts[2], lefts[3])], axis=1
+            )
+            right = jnp.concatenate(rights, axis=0)
+            totals[i] = totals[i] + jnp.dot(left, right, preferred_element_type=F32)
+    return [total[:64] + total[64:] for total in totals]
+
+
+def fold(both):
     return both + pltpu.roll(both, 64, 1)
 
 
-def ordered_products(sizes, codes, line, first, product, blocks, group, left_ref, right_ref, finish):
+def ordered_products(sizes, codes, line, first, product, blocks, left_ref, right_ref, sums, group=16):
     lane = product * sizes.pairs
     limits = (0, sizes.pairs // 2, 3 * sizes.pairs // 4, sizes.pairs)
 
@@ -145,13 +133,24 @@
 
             @pl.when((most > low) & (most <= high))
             def _():
-                for s in range(group):
-                    place = (codes[line + product, g * group + s] & (CODE - 1)) - first
-                    finish(place, fold(block_products(codes, place, lane, high, left_ref, right_ref)))
+                for s in range(0, group, 2):
+                    places = [(codes[line + product, g * group + s + i] & (CODE - 1)) - first for i in range(2)]
+                    totals = block_products(codes, places, lane, high, left_ref, right_ref)
+                    for place, total in zip(places, totals):
+                        sums[place] = total
 
         return carry
 
     lax.fori_loop(0, blocks // group, body, 0)
+
+
+def each(count, body, unroll=32):
+    def step(i, carry):
+        for s in range(unroll):
+            body(i * unroll + s)
+        return carry
+
+    lax.fori_loop(0, count // unroll, step, 0)
 
 
 def order_by_count(codes, lane, wanted, blocks):
@@ -210,7 +209,7 @@
 
 def first_step_kernel(sizes, offsets, *refs):
     pieces, refs = refs[: len(offsets)], refs[len(offsets) :]
-    out, codes_out, left_ref, right_ref, square_ref, squares, codes, sems = refs
+    out, codes_out, left_ref, right_ref, square_ref, squares, sums, codes, sems = refs
     row, col, rep = lax.axis_index("row"), lax.axis_index("col"), lax.axis_index("rep")
 
     def place_of(offset):
@@ -252,18 +251,21 @@
     for copy in copies:
         copy.wait()
 
-    def finish_square(place, twice):
+    def finish_square(place):
+        twice = fold(sums[place])
         store_left(square_ref, place, twice)
         squares[place] = pack(twice)
 
-    def finish_cube(place, twice):
-        out[place] = 3.0 * squares[place] - 2.0 * pack(twice)
-
-    ordered_products(sizes, codes, sizes.half, first, 0, sizes.half, 16, left_ref, right_ref, finish_square)
-    ordered_products(sizes, codes, sizes.half, first, 1, sizes.half, 16, square_ref, right_ref, finish_cube)
-
-
-def last_step_kernel(sizes, own, other, codes_in, out, left_ref, right_ref, square_ref, squares, codes, sems):
+    def finish_cube(place):
+        out[place] = 3.0 * squares[place] - 2.0 * pack(fold(sums[place]))
+
+    ordered_products(sizes, codes, sizes.half, first, 0, sizes.half, left_ref, right_ref, sums)
+    each(sizes.half, finish_square)
+    ordered_products(sizes, codes, sizes.half, first, 1, sizes.half, square_ref, right_ref, sums)
+    each(sizes.half, finish_cube)
+
+
+def last_step_kernel(sizes, own, other, codes_in, out, left_ref, right_ref, square_ref, squares, sums, codes, sems):
     row, col, rep = lax.axis_index("row"), lax.axis_index("col"), lax.axis_index("rep")
     first = pl.multiple_of(row * sizes.panel, sizes.panel)
     copies = [
@@ -274,16 +276,12 @@
         copy.start()
     zero_block(left_ref, sizes.panel, right_ref, sizes.blocks)
     zero_block(square_ref, sizes.panel, None, None)
-    unroll = 2 * sizes.slots
     for part, source in ((rep, own), (1 - rep, other)):
 
-        def prepare_right(i, carry):
-            for s in range(unroll):
-                at = i * unroll + s
-                store_right(right_ref, part * sizes.half + at, spread(source[at]))
-            return carry
-
-        lax.fori_loop(0, sizes.half // unroll, prepare_right, 0)
+        def prepare_right(at):
+            store_right(right_ref, part * sizes.half + at, spread(source[at]))
+
+        each(sizes.half, prepare_right)
 
         @pl.when(row // (sizes.rows // 2) == part)
         def _():
@@ -294,15 +292,19 @@
     for copy in copies:
         copy.wait()
 
-    def finish_square(place, twice):
+    def finish_square(place):
+        twice = fold(sums[place])
         store_left(square_ref, place, twice)
         squares[place] = pack(twice)
 
-    ordered_products(sizes, codes, sizes.panel, first, 2, sizes.panel, 16, left_ref, right_ref, finish_square)
+    ordered_products(sizes, codes, sizes.panel, first, 2, sizes.panel, left_ref, right_ref, sums)
+    each(sizes.panel, finish_square)
     base = (col * sizes.reps + rep) * sizes.slots
-    for s in range(sizes.slots):
-        cube = fold(block_products(codes, base + s, 3 * sizes.pairs, sizes.pairs, square_ref, right_ref))
-        out[s] = (3.0 * spread(squares[base + s]) - 2.0 * cube)[:, :64]
+    for s in range(0, sizes.slots, 2):
+        places = [base + s, base + s + 1]
+        totals = block_products(codes, places, 3 * sizes.pairs, sizes.pairs, square_ref, right_ref)
+        for i, place in enumerate(places):
+            out[s + i] = (3.0 * spread(squares[place]) - 2.0 * fold(totals[i]))[:, :64]
 
 
 def call(kernel, sizes, outs, in_specs, out_specs, scratch, limit=40):
@@ -328,6 +330,7 @@
             pltpu.VMEM((sizes.blocks + 1, 64, 128), BF16),
             pltpu.VMEM((blocks + 1, 128, 128), BF16),
             pltpu.VMEM((blocks, 32, 128), F32),
+            pltpu.VMEM((blocks, 64, 128), F32),
             pltpu.SMEM((blocks + 8, code_shape[1]), jnp.int32),
             pltpu.SemaphoreType.DMA((2,)),
         ]

time: 58.4 us -> 57.3 us (0.981)
  starting transfers between devices: 16.7 us -> 16.1 us
    pallas_call x1, Pallas kernels: 9.17 us -> 8.42 us  [whole_form(): call(last_step_kernel, sizes, jax.ShapeDtypeStruct(density.shape, F32), [...]
    ppermute x17, starting transfers between devices: 16.7 us -> 16.1 us  [swap(): return lax.ppermute(value, axes, [(i, i ^ mask) for i in range(size)])]
where the time goes in v3:
time: 57.3 us; the launch traced here: 57.4 us
  Pallas kernels  31.3 us (55%)
  starting transfers between devices  16.1 us (28%)
  waiting for transfers between devices  9.76 us (17%)
    pallas_call x1, Pallas kernels, whole_form(): call(lambda *args: first_step_kernel(args[0], offsets, *args[1:]), sizes,...  21.2 us
    ppermute x17, starting transfers between devices, swap(): return lax.ppermute(value, axes, [(i, i ^ mask) for i in range(size)])  16.1 us
    ppermute x17, waiting for transfers between devices, swap(): return lax.ppermute(value, axes, [(i, i ^ mask) for i in range(size)])  9.76 us
    pallas_call x1, Pallas kernels, whole_form(): call(last_step_kernel, sizes, jax.ShapeDtypeStruct(density.shape, F32), [...  8.42 us
    pallas_call x1, Pallas kernels, whole_form(): call(pack_kernel, sizes, jax.ShapeDtypeStruct((sizes.slots * 33, 128), F3...  1.74 us
  transfers between devices with their start and end apart: 17, of which 6 were waited for; matrix products, arithmetic and copies ran while one was open for 0% of the time, Pallas kernels for 0%

profile of v3, /device:TPU:0, one launch (start us, length us, event | category | flops | bytes accessed | tf_op | source)
XLA Modules:
  0.0 57.4 jit_solution(3964857513037967591)
XLA Ops:
  0.0 1.7 %shard_map.46 = f32[264,128]{1,0:T(8,128)} custom-call(f32[8,64,64]{2,1,0:T(8,128)} %density.1, s32[2,2,8,32]{3,2,1,0:T(8,128)} %left_index.1, s32[2,2,8,32]{3,2,1,0:T(8,128)} %right_index.1, s32[2,2,8]{2,1,0:T(2,128)} %pair_count.1), custom_call_target="tpu_custom_call" | custom-call | tf_op jit(solution)/shard_map/pallas_call | solution.py:338
  1.7 0.9 %collective-permute-start.14 = (f32[264,128]{1,0:T(8,128)}, f32[264,128]{1,0:T(8,128)S(1)}, u32[]{:S(2)}, u32[]{:S(2)}) collective-permute-start(f32[264,128]{1,0:T(8,128)} %shard_map.46), channel_id=1, source_target_pairs={{0,0},{1,1},{2,2},{3,3},{4,4},{5,5},{6,6},{7,7},{8,8},{9,9},{10,10... | collective-permute-start | bytes 405512 | tf_op jit(solution)/shard_map/ppermute | solution.py:355
  2.7 3.0 %collective-permute-start.10 = (f32[264,128]{1,0:T(8,128)}, f32[264,128]{1,0:T(8,128)S(1)}, u32[]{:S(2)}, u32[]{:S(2)}) collective-permute-start(f32[264,128]{1,0:T(8,128)} %shard_map.46), channel_id=1, source_target_pairs={{0,4},{4,0},{8,12},{12,8},{1,5},{5,1},{9,13},{13,9},{2,6},{6,2},{1... | collective-permute-start | bytes 405512 | tf_op jit(solution)/shard_map/ppermute | solution.py:355
  5.7 1.5 %collective-permute-start.8 = (f32[264,128]{1,0:T(8,128)}, f32[264,128]{1,0:T(8,128)S(1)}, u32[]{:S(2)}, u32[]{:S(2)}) collective-permute-start(f32[264,128]{1,0:T(8,128)} %shard_map.46), channel_id=1, source_target_pairs={{0,2},{2,0},{1,3},{3,1},{4,6},{6,4},{5,7},{7,5},{8,10},{10,8},{9,1... | collective-permute-start | bytes 405512 | tf_op jit(solution)/shard_map/ppermute | solution.py:355
  7.2 2.6 %collective-permute-start = (f32[264,128]{1,0:T(8,128)}, f32[264,128]{1,0:T(8,128)S(1)}, u32[]{:S(2)}, u32[]{:S(2)}) collective-permute-start(f32[264,128]{1,0:T(8,128)} %shard_map.46), channel_id=1, source_target_pairs={{0,8},{4,12},{8,0},{12,4},{1,9},{5,13},{9,1},{13,5},{2,10},{6,14},... | collective-permute-start | bytes 405512 | tf_op jit(solution)/shard_map/ppermute | solution.py:355
  9.8 0.0 collective-permute-done.14.args_15_
  9.8 0.0 collective-permute-start.15
  9.8 0.0 collective-permute-done.10.args_13_
  9.8 0.5 collective-permute-start.13
  10.3 2.5 %collective-permute-start.11 = (f32[264,128]{1,0:T(8,128)S(1)}, f32[264,128]{1,0:T(8,128)S(1)}, u32[]{:S(2)}, u32[]{:S(2)}) collective-permute-start(f32[264,128]{1,0:T(8,128)S(1)} %collective-permute-done.10.args_13_), channel_id=1, source_target_pairs={{0,2},{2,0},{1,3},{3,1},{4,6},{6,4},{5,7},{7,5},{8,10},{10,8},{9,1... | collective-permute-start | bytes 405512 | tf_op jit(solution)/shard_map/ppermute | solution.py:355
  12.8 0.0 collective-permute-done.8.args_9_
  12.8 0.2 collective-permute-start.9
  13.0 3.0 %collective-permute-done.args_7_ = f32[264,128]{1,0:T(8,128)S(1)} collective-permute-done((f32[264,128]{1,0:T(8,128)}, f32[264,128]{1,0:T(8,128)S(1)}, u32[]{:S(2)}, u32[]{:S(2)}) %collective-permute-start) | collective-permute-done | bytes 135200 | tf_op jit(solution)/shard_map/ppermute | solution.py:355
  16.0 0.0 collective-permute-start.5
  16.0 0.0 collective-permute-done.15.args_14_
  16.0 0.8 %collective-permute-start.3 = (f32[264,128]{1,0:T(8,128)S(1)}, f32[264,128]{1,0:T(8,128)S(1)}, u32[]{:S(2)}, u32[]{:S(2)}) collective-permute-start(f32[264,128]{1,0:T(8,128)S(1)} %collective-permute-done.args_7_), channel_id=1, source_target_pairs={{0,2},{2,0},{1,3},{3,1},{4,6},{6,4},{5,7},{7,5},{8,10},{10,8},{9,1... | collective-permute-start | bytes 405512 | tf_op jit(solution)/shard_map/ppermute | solution.py:355
  16.7 0.0 collective-permute-done.13.args_12_
  16.7 2.7 %collective-permute-start.1 = (f32[264,128]{1,0:T(8,128)S(1)}, f32[264,128]{1,0:T(8,128)S(1)}, u32[]{:S(2)}, u32[]{:S(2)}) collective-permute-start(f32[264,128]{1,0:T(8,128)S(1)} %collective-permute-done.args_7_), channel_id=1, source_target_pairs={{0,6},{2,4},{4,2},{6,0},{8,14},{10,12},{12,10},{14,8},{1,7},{3,5},... | collective-permute-start | bytes 405512 | tf_op jit(solution)/shard_map/ppermute | solution.py:355
  19.5 0.0 collective-permute-done.11.args_11_
  19.5 0.0 collective-permute-start.7
  19.5 0.0 collective-permute-done.9.args_8_
  19.5 0.5 collective-permute-start.12
  20.0 2.0 %collective-permute-done.5.args_5_ = f32[264,128]{1,0:T(8,128)S(1)} collective-permute-done((f32[264,128]{1,0:T(8,128)S(1)}, f32[264,128]{1,0:T(8,128)S(1)}, u32[]{:S(2)}, u32[]{:S(2)}) %collective-permute-start.5) | collective-permute-done | bytes 135200 | tf_op jit(solution)/shard_map/ppermute | solution.py:355
  21.9 0.0 collective-permute-start.6
  21.9 1.5 %collective-permute-done.3.args_3_ = f32[264,128]{1,0:T(8,128)S(1)} collective-permute-done((f32[264,128]{1,0:T(8,128)S(1)}, f32[264,128]{1,0:T(8,128)S(1)}, u32[]{:S(2)}, u32[]{:S(2)}) %collective-permute-start.3) | collective-permute-done | bytes 135200 | tf_op jit(solution)/shard_map/ppermute | solution.py:355
  23.4 0.0 collective-permute-start.4
  23.4 0.0 collective-permute-done.1.args_1_
  23.4 0.5 collective-permute-start.2
  23.9 0.0 collective-permute-done.7.args_6_
  23.9 0.0 collective-permute-done.12.args_10_
  23.9 0.0 collective-permute-done.6.args_4_
  23.9 0.8 %collective-permute-done.4.args_2_ = f32[264,128]{1,0:T(8,128)S(1)} collective-permute-done((f32[264,128]{1,0:T(8,128)S(1)}, f32[264,128]{1,0:T(8,128)S(1)}, u32[]{:S(2)}, u32[]{:S(2)}) %collective-permute-start.4) | collective-permute-done | bytes 135200 | tf_op jit(solution)/shard_map/ppermute | solution.py:355
  24.7 0.2 collective-permute-done.2.args_0_
  24.9 21.2 %shard_map.47 = (f32[64,32,128]{2,1,0:T(8,128)S(1)}, s32[136,128]{1,0:T(8,128)S(1)}) custom-call(f32[264,128]{1,0:T(8,128)S(1)} %collective-permute-done.2.args_0_, f32[264,128]{1,0:T(8,128)S(1)} %collective-permute-done.1.args_1_, f32[264,128]{1,0:T(8,128)S(1)} %collective-permute-done.4.args_2_, f32[264,128]{1,0:T(8,128)S(1)} %collective-permute-done.3.args_3_, ...), custom_call_target="tpu_custom_call" | custom-call | tf_op jit(solution)/shard_map/pallas_call | solution.py:381
  46.1 0.4 collective-permute-start.16
  46.5 2.3 %collective-permute-done.16.other = f32[64,32,128]{2,1,0:T(8,128)S(1)} collective-permute-done((f32[64,32,128]{2,1,0:T(8,128)S(1)}, f32[64,32,128]{2,1,0:T(8,128)S(1)}, u32[]{:S(2)}, u32[]{:S(2)}) %collective-permute-start.16) | collective-permute-done | bytes 1048608 | tf_op jit(solution)/shard_map/ppermute | solution.py:355
  48.8 8.4 %shard_map.48 = f32[8,64,64]{2,1,0:T(8,128)} custom-call(f32[64,32,128]{2,1,0:T(8,128)S(1)} %get-tuple-element.7.own, f32[64,32,128]{2,1,0:T(8,128)S(1)} %collective-permute-done.16.other, s32[136,128]{1,0:T(8,128)S(1)} %get-tuple-element.8.codes_in), custom_call_target="tpu_custom_call" | custom-call | tf_op jit(solution)/shard_map/pallas_call | solution.py:389
Async XLA Ops:
  1.7 8.0 %collective-permute-start.14 = (f32[264,128]{1,0:T(8,128)}, f32[264,128]{1,0:T(8,128)S(1)}, u32[]{:S(2)}, u32[]{:S(2)}) collective-permute-start(f32[264,128]{1,0:T(8,128)} %shard_map.46), channel_id=1, source_target_pairs={{0,0},{1,1},{2,2},{3,3},{4,4},{5,5},{6,6},{7,7},{8,8},{9,9},{10,10... | collective-permute-start | bytes 405512 | tf_op jit(solution)/shard_map/ppermute | solution.py:355
  2.7 7.1 %collective-permute-start.10 = (f32[264,128]{1,0:T(8,128)}, f32[264,128]{1,0:T(8,128)S(1)}, u32[]{:S(2)}, u32[]{:S(2)}) collective-permute-start(f32[264,128]{1,0:T(8,128)} %shard_map.46), channel_id=1, source_target_pairs={{0,4},{4,0},{8,12},{12,8},{1,5},{5,1},{9,13},{13,9},{2,6},{6,2},{1... | collective-permute-start | bytes 405512 | tf_op jit(solution)/shard_map/ppermute | solution.py:355
  5.7 7.1 %collective-permute-start.8 = (f32[264,128]{1,0:T(8,128)}, f32[264,128]{1,0:T(8,128)S(1)}, u32[]{:S(2)}, u32[]{:S(2)}) collective-permute-start(f32[264,128]{1,0:T(8,128)} %shard_map.46), channel_id=1, source_target_pairs={{0,2},{2,0},{1,3},{3,1},{4,6},{6,4},{5,7},{7,5},{8,10},{10,8},{9,1... | collective-permute-start | bytes 405512 | tf_op jit(solution)/shard_map/ppermute | solution.py:355
  7.2 8.8 %collective-permute-start = (f32[264,128]{1,0:T(8,128)}, f32[264,128]{1,0:T(8,128)S(1)}, u32[]{:S(2)}, u32[]{:S(2)}) collective-permute-start(f32[264,128]{1,0:T(8,128)} %shard_map.46), channel_id=1, source_target_pairs={{0,8},{4,12},{8,0},{12,4},{1,9},{5,13},{9,1},{13,5},{2,10},{6,14},... | collective-permute-start | bytes 405512 | tf_op jit(solution)/shard_map/ppermute | solution.py:355
  9.8 6.2 %collective-permute-start.15 = (f32[264,128]{1,0:T(8,128)S(1)}, f32[264,128]{1,0:T(8,128)S(1)}, u32[]{:S(2)}, u32[]{:S(2)}) collective-permute-start(f32[264,128]{1,0:T(8,128)S(1)} %collective-permute-done.14.args_15_), channel_id=1, source_target_pairs={{0,1},{1,0},{2,3},{3,2},{4,5},{5,4},{6,7},{7,6},{8,9},{9,8},{10,11... | collective-permute-start | bytes 405512 | tf_op jit(solution)/shard_map/ppermute | solution.py:355
  9.8 7.0 %collective-permute-start.13 = (f32[264,128]{1,0:T(8,128)S(1)}, f32[264,128]{1,0:T(8,128)S(1)}, u32[]{:S(2)}, u32[]{:S(2)}) collective-permute-start(f32[264,128]{1,0:T(8,128)S(1)} %collective-permute-done.10.args_13_), channel_id=1, source_target_pairs={{0,1},{1,0},{2,3},{3,2},{4,5},{5,4},{6,7},{7,6},{8,9},{9,8},{10,11... | collective-permute-start | bytes 405512 | tf_op jit(solution)/shard_map/ppermute | solution.py:355
  10.3 9.2 %collective-permute-start.11 = (f32[264,128]{1,0:T(8,128)S(1)}, f32[264,128]{1,0:T(8,128)S(1)}, u32[]{:S(2)}, u32[]{:S(2)}) collective-permute-start(f32[264,128]{1,0:T(8,128)S(1)} %collective-permute-done.10.args_13_), channel_id=1, source_target_pairs={{0,2},{2,0},{1,3},{3,1},{4,6},{6,4},{5,7},{7,5},{8,10},{10,8},{9,1... | collective-permute-start | bytes 405512 | tf_op jit(solution)/shard_map/ppermute | solution.py:355
  12.8 6.7 %collective-permute-start.9 = (f32[264,128]{1,0:T(8,128)S(1)}, f32[264,128]{1,0:T(8,128)S(1)}, u32[]{:S(2)}, u32[]{:S(2)}) collective-permute-start(f32[264,128]{1,0:T(8,128)S(1)} %collective-permute-done.8.args_9_), channel_id=1, source_target_pairs={{0,1},{1,0},{2,3},{3,2},{4,5},{5,4},{6,7},{7,6},{8,9},{9,8},{10,11... | collective-permute-start | bytes 405512 | tf_op jit(solution)/shard_map/ppermute | solution.py:355
  16.0 6.0 %collective-permute-start.5 = (f32[264,128]{1,0:T(8,128)S(1)}, f32[264,128]{1,0:T(8,128)S(1)}, u32[]{:S(2)}, u32[]{:S(2)}) collective-permute-start(f32[264,128]{1,0:T(8,128)S(1)} %collective-permute-done.args_7_), channel_id=1, source_target_pairs={{0,4},{4,0},{8,12},{12,8},{1,5},{5,1},{9,13},{13,9},{2,6},{6,2},{1... | collective-permute-start | bytes 405512 | tf_op jit(solution)/shard_map/ppermute | solution.py:355
  16.0 7.4 %collective-permute-start.3 = (f32[264,128]{1,0:T(8,128)S(1)}, f32[264,128]{1,0:T(8,128)S(1)}, u32[]{:S(2)}, u32[]{:S(2)}) collective-permute-start(f32[264,128]{1,0:T(8,128)S(1)} %collective-permute-done.args_7_), channel_id=1, source_target_pairs={{0,2},{2,0},{1,3},{3,1},{4,6},{6,4},{5,7},{7,5},{8,10},{10,8},{9,1... | collective-permute-start | bytes 405512 | tf_op jit(solution)/shard_map/ppermute | solution.py:355
  16.7 6.7 %collective-permute-start.1 = (f32[264,128]{1,0:T(8,128)S(1)}, f32[264,128]{1,0:T(8,128)S(1)}, u32[]{:S(2)}, u32[]{:S(2)}) collective-permute-start(f32[264,128]{1,0:T(8,128)S(1)} %collective-permute-done.args_7_), channel_id=1, source_target_pairs={{0,6},{2,4},{4,2},{6,0},{8,14},{10,12},{12,10},{14,8},{1,7},{3,5},... | collective-permute-start | bytes 405512 | tf_op jit(solution)/shard_map/ppermute | solution.py:355
  19.5 4.4 %collective-permute-start.7 = (f32[264,128]{1,0:T(8,128)S(1)}, f32[264,128]{1,0:T(8,128)S(1)}, u32[]{:S(2)}, u32[]{:S(2)}) collective-permute-start(f32[264,128]{1,0:T(8,128)S(1)} %collective-permute-done.args_7_), channel_id=1, source_target_pairs={{0,1},{1,0},{2,3},{3,2},{4,5},{5,4},{6,7},{7,6},{8,9},{9,8},{10,11... | collective-permute-start | bytes 405512 | tf_op jit(solution)/shard_map/ppermute | solution.py:355
  19.5 4.4 %collective-permute-start.12 = (f32[264,128]{1,0:T(8,128)S(1)}, f32[264,128]{1,0:T(8,128)S(1)}, u32[]{:S(2)}, u32[]{:S(2)}) collective-permute-start(f32[264,128]{1,0:T(8,128)S(1)} %collective-permute-done.11.args_11_), channel_id=1, source_target_pairs={{0,1},{1,0},{2,3},{3,2},{4,5},{5,4},{6,7},{7,6},{8,9},{9,8},{10,11... | collective-permute-start | bytes 405512 | tf_op jit(solution)/shard_map/ppermute | solution.py:355
  21.9 2.0 %collective-permute-start.6 = (f32[264,128]{1,0:T(8,128)S(1)}, f32[264,128]{1,0:T(8,128)S(1)}, u32[]{:S(2)}, u32[]{:S(2)}) collective-permute-start(f32[264,128]{1,0:T(8,128)S(1)} %collective-permute-done.5.args_5_), channel_id=1, source_target_pairs={{0,1},{1,0},{2,3},{3,2},{4,5},{5,4},{6,7},{7,6},{8,9},{9,8},{10,11... | collective-permute-start | bytes 405512 | tf_op jit(solution)/shard_map/ppermute | solution.py:355
  23.4 1.4 %collective-permute-start.4 = (f32[264,128]{1,0:T(8,128)S(1)}, f32[264,128]{1,0:T(8,128)S(1)}, u32[]{:S(2)}, u32[]{:S(2)}) collective-permute-start(f32[264,128]{1,0:T(8,128)S(1)} %collective-permute-done.3.args_3_), channel_id=1, source_target_pairs={{0,1},{1,0},{2,3},{3,2},{4,5},{5,4},{6,7},{7,6},{8,9},{9,8},{10,11... | collective-permute-start | bytes 405512 | tf_op jit(solution)/shard_map/ppermute | solution.py:355
  23.4 1.5 %collective-permute-start.2 = (f32[264,128]{1,0:T(8,128)S(1)}, f32[264,128]{1,0:T(8,128)S(1)}, u32[]{:S(2)}, u32[]{:S(2)}) collective-permute-start(f32[264,128]{1,0:T(8,128)S(1)} %collective-permute-done.1.args_1_), channel_id=1, source_target_pairs={{0,1},{1,0},{2,3},{3,2},{4,5},{5,4},{6,7},{7,6},{8,9},{9,8},{10,11... | collective-permute-start | bytes 405512 | tf_op jit(solution)/shard_map/ppermute | solution.py:355
  46.1 2.7 %collective-permute-start.16 = (f32[64,32,128]{2,1,0:T(8,128)S(1)}, f32[64,32,128]{2,1,0:T(8,128)S(1)}, u32[]{:S(2)}, u32[]{:S(2)}) collective-permute-start(f32[64,32,128]{2,1,0:T(8,128)S(1)} %get-tuple-element.7.own), channel_id=1, source_target_pairs={{0,1},{1,0},{2,3},{3,2},{4,5},{5,4},{6,7},{7,6},{8,9},{9,8},{10,11... | collective-permute-start | bytes 3145736 | tf_op jit(solution)/shard_map/ppermute | solution.py:355
